TPU v7x, 128 devices: a whole 4x4x4 slice. The times are simulated.
128 devices in a mesh: gr: 16 (over z, y_hi, core), gc: 8 (over x, y_lo).
Axes of the slice: x: 4, y: 4 (y_hi: 2, y_lo: 2; y = y_hi * 2 + y_lo), z: 4, core: 2. Of those that a mesh axis runs over, the one named last changes fastest.
Arguments:
- right_sides: float32 [131072, 1024], P('gr', 'gc'), may hold values from -6 to 6
- factor_panel: bfloat16 [3, 131072, 1024], P(None, ('gr', 'gc')), may hold values from -0.1875 to 0.1875
- diag_inverse: bfloat16 [3, 1024, 1024], replicated, as said below
- block_ids: int32 [128], replicated, may hold values from 0 to 127, each once
- step_blocks: int32 [3], replicated, may hold values from 0 to 33, as said below
Outputs:
- solved_rhs: float32 [131072, 1024], P('gr', 'gc')
Inputs may be any that keep to these rules, and one draw needn't show every extreme that they name: `block_ids`: each number appears once. `step_blocks`: 3 distinct rising block numbers, the first 0 and the last 33. `diag_inverse`: lower triangular with a positive diagonal.
All inputs are finite; a program needn't handle non-finite values.
Results may differ from a plain program's by a relative error of at most 0.0059.
Values may be sent and summed in bfloat16 or wider, within the bound.
A program may use at most 128 MiB of HBM per device.

v0:
```python
import jax
import jax.numpy as jnp
from jax import lax
from jax.sharding import PartitionSpec as P


def from_root(shard, axis, root):
    mine = lax.axis_index(axis) == root
    return lax.psum(jnp.where(mine, shard, jnp.zeros_like(shard)), axis)


def subtract_pending(current, arrived, pending, per_row, block_rows):
    shaped = current.reshape(per_row, block_rows, current.shape[1])
    incoming = arrived.reshape(per_row, block_rows, current.shape[1]).astype(jnp.float32)
    shaped = shaped - jnp.where(pending[:, None, None], incoming, 0.0)
    return shaped.reshape(current.shape)


def shards(right_sides, factor_panel, diag_inverse, block_ids, step_blocks):
    block_rows = diag_inverse.shape[1]
    rows_dev = factor_panel.shape[1]
    per_dev = rows_dev // block_rows
    columns = lax.axis_size("gc")
    per_row = per_dev * columns
    row_here = lax.axis_index("gr")
    block_count = block_ids.shape[0]
    numbering = jnp.arange(block_count, dtype=jnp.int32)
    local_ids = lax.dynamic_slice_in_dim(block_ids, row_here * per_row, per_row, 0)
    current = right_sides
    solved = []
    block_list = []
    for step in range(diag_inverse.shape[0]):
        block_no = step_blocks[step]
        block_list.append(block_no)
        position = jnp.sum(jnp.where(block_ids == block_no, numbering, 0))
        owner_row = position // per_row
        in_row = position % per_row
        target = lax.dynamic_slice_in_dim(current, in_row * block_rows, block_rows, 0)
        y_part = jnp.dot(
            diag_inverse[step].astype(jnp.float32), target, precision=lax.Precision.HIGHEST
        )
        solved.append((owner_row, in_row, y_part))
        panel_step = factor_panel[step]
        row_y = lax.all_gather(y_part.astype(jnp.bfloat16), "gc", axis=1, tiled=True).astype(
            y_part.dtype
        )
        full_y = from_root(row_y.astype(jnp.bfloat16), "gr", owner_row).astype(row_y.dtype)
        contrib = jnp.dot(
            panel_step, full_y.astype(jnp.bfloat16), preferred_element_type=jnp.float32
        ).astype(jnp.bfloat16)
        arrived_rows = lax.all_to_all(contrib, "gc", split_axis=1, concat_axis=0, tiled=True)
        current = subtract_pending(current, arrived_rows, local_ids > block_no, per_row, block_rows)
    for owner_row, in_row, y_part in solved:
        written = lax.dynamic_update_slice_in_dim(current, y_part, in_row * block_rows, 0)
        current = jnp.where(row_here == owner_row, written, current)
    return current


def solution(mesh):
    in_specs = (P("gr", "gc"), P(None, ("gr", "gc"), None), P(), P(), P())
    out_specs = P("gr", "gc")
    return jax.shard_map(shards, mesh=mesh, in_specs=in_specs, out_specs=out_specs, check_vma=False)
```

profile of v0, /device:TPU:0, one launch (start us, length us, event | category | flops | bytes accessed | tf_op | source)
XLA Modules:
  0.0 772.9 jit_solution(16256889289489155128)
XLA Ops:
  6.5 1.4 fusion.45
  8.0 3.4 fusion.44
  13.0 4.7 fusion.46
  17.8 0.0 all-reduce.4.cloned.1.call-start
  18.5 53.1 %all-gather.4.cloned.1.call-done = bf16[1024,1024]{0,1:T(8,128)(2,1)} async-done(((bf16[1024,128]{0,1:T(8,128)(2,1)}), bf16[1024,1024]{0,1:T(8,128)(2,1)}) %all-gather.4.cloned.1.call-update) | async-done | bytes 2097168 | tf_op jit(solution)/shard_map/all_gather | solution.py:44
  71.5 1.5 broadcast_select_fusion.2
  73.0 147.9 %all-reduce.4.cloned.1.call-done = bf16[1024,1024]{0,1:T(8,128)(2,1)} async-done(((bf16[1024,1024]{0,1:T(8,128)(2,1)}), bf16[1024,1024]{0,1:T(8,128)(2,1)}) %all-reduce.4.cloned.1.call-update) | async-done | bytes 2097168 | tf_op jit(solution)/shard_map/psum | solution.py:9
  220.9 5.9 fusion.18
  226.8 4.3 all-to-all-start
  233.1 5.6 copy.12
  238.7 2.1 broadcast_compare_fusion
  240.7 0.1 broadcast_bitcast_fusion.2
  240.8 19.5 %all-to-all-done = bf16[1024,8,128]{0,2,1:T(8,128)(2,1)S(1)} async-done(((bf16[1024,8,128]{0,2,1:T(8,128)(2,1)}), bf16[1024,8,128]{0,2,1:T(8,128)(2,1)S(1)}, u32[]{:S(2)}, u32[]{:S(2)}) %all-to-all-start) | async-done | bytes 2097184 | tf_op jit(solution)/shard_map/all_to_all | solution.py:51
  260.3 0.5 convert_bitcast_fusion.2
  260.8 0.3 copy.16
  261.1 1.9 copy-done.4
  263.0 0.5 select_subtract_fusion.2
  263.5 2.0 copy-done
  265.5 4.5 fusion.47
  270.7 45.5 %all-gather.6.cloned.1.call-done = bf16[1024,1024]{0,1:T(8,128)(2,1)} async-done(((bf16[1024,128]{0,1:T(8,128)(2,1)}), bf16[1024,1024]{0,1:T(8,128)(2,1)}) %all-gather.6.cloned.1.call-update) | async-done | bytes 2097168 | tf_op jit(solution)/shard_map/all_gather | solution.py:44
  316.3 1.5 broadcast_select_fusion.1
  317.7 147.7 %all-reduce.6.cloned.1.call-done = bf16[1024,1024]{0,1:T(8,128)(2,1)} async-done(((bf16[1024,1024]{0,1:T(8,128)(2,1)}), bf16[1024,1024]{0,1:T(8,128)(2,1)}) %all-reduce.6.cloned.1.call-update) | async-done | bytes 2097168 | tf_op jit(solution)/shard_map/psum | solution.py:9
  465.5 5.9 fusion.21
  471.4 4.3 all-to-all-start.1
  475.6 0.2 all-gather.8.cloned.1.call-start
  478.0 0.1 broadcast_bitcast_fusion.1
  478.0 26.8 %all-to-all-done.1 = bf16[1024,8,128]{0,2,1:T(8,128)(2,1)S(1)} async-done(((bf16[1024,8,128]{0,2,1:T(8,128)(2,1)}), bf16[1024,8,128]{0,2,1:T(8,128)(2,1)S(1)}, u32[]{:S(2)}, u32[]{:S(2)}) %all-to-all-start.1) | async-done | bytes 2097184 | tf_op jit(solution)/shard_map/all_to_all | solution.py:51
  504.9 0.5 convert_bitcast_fusion.1
  505.4 0.3 copy.17
  505.7 1.9 copy-done.1
  507.5 0.5 select_subtract_fusion.1
  508.1 2.0 copy-done.2
  510.1 4.7 fusion.48
  515.6 45.5 %all-gather.8.cloned.1.call-done = bf16[1024,1024]{0,1:T(8,128)(2,1)} async-done(((bf16[1024,128]{0,1:T(8,128)(2,1)}), bf16[1024,1024]{0,1:T(8,128)(2,1)}) %all-gather.8.cloned.1.call-update) | async-done | bytes 2097168 | tf_op jit(solution)/shard_map/all_gather | solution.py:44
  561.0 1.5 broadcast_select_fusion
  562.5 147.7 %all-reduce.8.cloned.1.call-done = bf16[1024,1024]{0,1:T(8,128)(2,1)} async-done(((bf16[1024,1024]{0,1:T(8,128)(2,1)}), bf16[1024,1024]{0,1:T(8,128)(2,1)}) %all-reduce.8.cloned.1.call-update) | async-done | bytes 2097168 | tf_op jit(solution)/shard_map/psum | solution.py:9
  710.2 5.9 fusion.24
  716.1 4.3 all-to-all-start.2
  720.4 0.1 broadcast_bitcast_fusion
  720.5 29.1 %all-to-all-done.2 = bf16[1024,8,128]{0,2,1:T(8,128)(2,1)S(1)} async-done(((bf16[1024,8,128]{0,2,1:T(8,128)(2,1)}), bf16[1024,8,128]{0,2,1:T(8,128)(2,1)S(1)}, u32[]{:S(2)}, u32[]{:S(2)}) %all-to-all-start.2) | async-done | bytes 2097184 | tf_op jit(solution)/shard_map/all_to_all | solution.py:51
  749.6 0.5 convert_bitcast_fusion
  750.1 0.3 copy.18
  750.4 1.9 copy-done.3
  752.3 2.4 select_subtract_fusion
  754.7 1.9 select_dynamic-update-slice_fusion.2
  756.6 1.9 select_dynamic-update-slice_fusion.1
  758.5 1.9 select_dynamic-update-slice_fusion
  760.4 5.6 copy.15
  (22 shorter events, 0.3 us)
Async XLA Ops:
  6.5 65.0 %all-gather.4.cloned.1.call-start = ((), (), s32[]{:S(2)}) async-start(), calls=%async_computation.3 | async-start | bytes 2359296 | tf_op jit(solution)/shard_map/all_gather | solution.py:44
  17.8 203.1 %all-reduce.4.cloned.1.call-start = ((), (), s32[]{:S(2)}) async-start(), calls=%async_computation.4 | async-start | bytes 4194304 | tf_op jit(solution)/shard_map/psum | solution.py:9
  226.8 33.5 %all-to-all-start = ((bf16[1024,8,128]{0,2,1:T(8,128)(2,1)}), bf16[1024,8,128]{0,2,1:T(8,128)(2,1)S(1)}, u32[]{:S(2)}, u32[]{:S(2)}) async-start(bf16[1024,8,128]{0,2,1:T(8,128)(2,1)} %bitcast.87), calls=%async_computation | async-start | bytes 4194304 | tf_op jit(solution)/shard_map/all_to_all | solution.py:51
  231.1 85.2 %all-gather.6.cloned.1.call-start = ((), (), s32[]{:S(2)}) async-start(), calls=%async_computation.5 | async-start | bytes 2359296 | tf_op jit(solution)/shard_map/all_gather | solution.py:44
  233.1 5.6 copy-start.6
  260.8 2.2 copy-start.4
  263.5 2.0 copy-start
  270.0 195.4 %all-reduce.6.cloned.1.call-start = ((), (), s32[]{:S(2)}) async-start(), calls=%async_computation.6 | async-start | bytes 4194304 | tf_op jit(solution)/shard_map/psum | solution.py:9
  471.4 33.5 %all-to-all-start.1 = ((bf16[1024,8,128]{0,2,1:T(8,128)(2,1)}), bf16[1024,8,128]{0,2,1:T(8,128)(2,1)S(1)}, u32[]{:S(2)}, u32[]{:S(2)}) async-start(bf16[1024,8,128]{0,2,1:T(8,128)(2,1)} %bitcast.88), calls=%async_computation.1 | async-start | bytes 4194304 | tf_op jit(solution)/shard_map/all_to_all | solution.py:51
  475.6 85.4 %all-gather.8.cloned.1.call-start = ((), (), s32[]{:S(2)}) async-start(), calls=%async_computation.7 | async-start | bytes 2359296 | tf_op jit(solution)/shard_map/all_gather | solution.py:44
  505.3 2.2 copy-start.1
  508.1 2.0 copy-start.2
  514.8 195.4 %all-reduce.8.cloned.1.call-start = ((), (), s32[]{:S(2)}) async-start(), calls=%async_computation.8 | async-start | bytes 4194304 | tf_op jit(solution)/shard_map/psum | solution.py:9
  716.1 33.5 %all-to-all-start.2 = ((bf16[1024,8,128]{0,2,1:T(8,128)(2,1)}), bf16[1024,8,128]{0,2,1:T(8,128)(2,1)S(1)}, u32[]{:S(2)}, u32[]{:S(2)}) async-start(bf16[1024,8,128]{0,2,1:T(8,128)(2,1)} %bitcast.89), calls=%async_computation.2 | async-start | bytes 4194304 | tf_op jit(solution)/shard_map/all_to_all | solution.py:51
  750.1 2.2 copy-start.3
  752.3 6.2 copy-start.5
Sparse Core Ops, SparseCore 0:
  17.9 53.5 all-gather.3
  74.0 146.8 all-reduce.3
  270.1 46.0 all-gather.5
  318.6 146.8 all-reduce.5
  514.9 46.0 all-gather.7
  563.4 146.8 all-reduce.7
where the time goes:
time: 775 us; the launch traced here: 773 us
  waiting for transfers between devices  663 us (86%)
  matrix products  31.6 us (4%)
  local copies, waits for them, and re-layouts  23.4 us (3%)
  between operations  21.3 us (3%)
  other arithmetic  20.4 us (3%)
  starting transfers between devices  13.2 us (2%)
    psum x3, waiting for transfers between devices, from_root(): return lax.psum(jnp.where(mine, shard, jnp.zeros_like(shard)), axis)  443 us
    all_gather x3, waiting for transfers between devices, shards(): lax.all_gather(y_part.astype(jnp.bfloat16), 'gc', axis=1, tiled=True)  144 us
    all_to_all x3, waiting for transfers between devices, shards(): lax.all_to_all(contrib, 'gc', split_axis=1, concat_axis=0, tiled=True)  75.4 us
    dot_general x3, matrix products, shards(): jnp.dot(panel_step, full_y.astype(jnp.bfloat16), preferred_element_type=j...  17.8 us
    unnamed x21, local copies, waits for them, and re-layouts  15.5 us
  transfers between devices with their start and end apart: 9, of which 9 were waited for; matrix products, arithmetic and copies ran while one was open for 1% of the time, Pallas kernels for 0%

commit v1 on v0

v1 whole, which is shorter than its diff:
```python
import jax
import jax.numpy as jnp
from jax import lax
from jax.experimental import pallas as pl
from jax.experimental.pallas import tpu as pltpu
from jax.sharding import PartitionSpec as P

MESH = pl.DeviceIdType.MESH
F32 = jnp.float32
BF16 = jnp.bfloat16
NB = 1024
HALF = 512
COLS = 128
ROW_PEERS = ((0, 1), (1, 0), (3, 0), (1, 1), (3, 1), (2, 0), (2, 1))
INVERSE = tuple(ROW_PEERS.index(((4 - dx) % 4, flip)) for dx, flip in ROW_PEERS)
ORDERS = ((0, 1, 2), (1, 2, 0), (2, 0, 1))


def dot(a, b):
    return jnp.dot(a, b, preferred_element_type=F32)


def kernel(
    flags, rhs_ref, panel_ref, diag_ref, out_ref,
    rhs, panel, diag, fin, w, w2, r1, r2, r3,
    thl, a0, stage, a_in, a_half, a_z, a_piece, a_y, afull,
    yf, ysol, g0_out, g0_in, g1_out, g1_in, acc, c_out, c_in,
    load_sem, out_sem, fin_s, fin_r, sel_s, sel_r, a_s, a_r, y_s, y_r, fw_s, fw_r, g_s, g_r, c_s, c_r,
):
    gr, gc = lax.axis_index("gr"), lax.axis_index("gc")
    z, y_hi, core = gr // 4, (gr // 2) % 2, gr % 2
    x, y_lo = gc // 2, gc % 2
    y = y_hi * 2 + y_lo
    other = 1 - core
    here = (x, y, z)

    def device(at, c):
        return (at[2] * 4 + (at[1] // 2) * 2 + c, at[0] * 2 + at[1] % 2)

    def along(axis, step):
        at = list(here)
        at[axis] = (at[axis] + step) % 4
        return device(at, core)

    def row_peer(i, sign):
        dx, flip = ROW_PEERS[i]
        return ((x + sign * dx + 4) % 4) * 2 + (y_lo + flip) % 2

    def send(src, dst, s, r, to):
        copy = pltpu.make_async_remote_copy(
            src_ref=src, dst_ref=dst, send_sem=s, recv_sem=r, device_id=to, device_id_type=MESH
        )
        copy.start()
        return copy

    def local(src, dst, sem):
        copy = pltpu.make_async_copy(src, dst, sem)
        copy.start()
        return copy

    partner = (gr + 1 - 2 * core, gc)
    mine = pl.ds(pl.multiple_of(core * HALF, HALF), HALF)
    theirs = pl.ds(pl.multiple_of(other * HALF, HALF), HALF)

    load_f = [local(panel_ref.at[t], panel.at[t], load_sem.at[t]) for t in range(2)]
    load_rhs = local(rhs_ref, rhs, load_sem.at[3])
    load_d = local(diag_ref, diag, load_sem.at[4])
    load_f.append(local(panel_ref.at[2], panel.at[2], load_sem.at[2]))

    peers = [along(axis, step) for axis in range(3) for step in (1, 2, 3)]
    peers += [(gr, row_peer(i, 1)) for i in (3, 4, 6)] + [partner]
    barrier = pltpu.get_barrier_semaphore()
    for peer in peers:
        pl.semaphore_signal(barrier, inc=1, device_id=peer, device_id_type=MESH)
    pl.semaphore_wait(barrier, len(peers))

    fin_copies = []
    for t in range(2):
        for h in range(2):
            i = t * 2 + h
            fin_copies.append(
                send(
                    panel_ref.at[t, theirs, pl.ds(h * HALF, HALF)],
                    fin.at[t, pl.ds(h * HALF, HALF)],
                    fin_s.at[i], fin_r.at[i], partner,
                )
            )

    def flag(row):
        return flags[row:row + 1, :]

    def build(slot, t, row):
        def mask(r):
            tile = jnp.broadcast_to(flag(r), (128, COLS)).astype(BF16)
            return jnp.concatenate([tile] * (HALF // COLS), axis=1)

        own, oth = mask(row), mask(row + 1)

        def chunk(i, carry):
            rows = pl.ds(pl.multiple_of(core * HALF + i * 128, 128), 128)
            for h in range(2):
                to = pl.ds(pl.multiple_of(h * HALF + i * 128, 128), 128)
                w[slot, to] = panel[t, rows, pl.ds(h * HALF, HALF)] * own + fin[t, to] * oth
            return carry

        lax.fori_loop(0, 4, chunk, 0)

    bases = []
    for slot in range(3):
        v = [here[a] for a in ORDERS[slot]]
        bases.append((v, (0, v[0] * 256, v[0] * 256 + v[1] * 64)))
    sizes = (256, 64, 16)

    def sem_at(slot, stage_no, step):
        return (slot * 6 + stage_no) * 3 + step - 1

    def scatter(slot, st):
        v, base = bases[slot]
        size = sizes[st]
        buf = (r1, r2, r3)[st]
        out = []
        for step in (1, 2, 3):
            rows = pl.ds(pl.multiple_of(base[st] + ((v[st] + step) % 4) * size, size), size)
            i = sem_at(slot, st, step)
            out.append(
                send(
                    w.at[slot, rows], buf.at[slot, step - 1], sel_s.at[i], sel_r.at[i],
                    along(ORDERS[slot][st], step),
                )
            )
        return out

    def total(slot, st, copies):
        v, base = bases[slot]
        size = sizes[st]
        buf = (r1, r2, r3)[st]
        for copy in copies:
            copy.wait()
        start = base[st] + v[st] * size
        span = min(size, 64)

        def chunk(i, carry):
            rows = pl.ds(pl.multiple_of(start + i * span, span), span)
            part = pl.ds(pl.multiple_of(i * span, span), span)
            value = w[slot, rows] + buf[slot, 0, part] + (buf[slot, 1, part] + buf[slot, 2, part])
            if st == 2:
                w2[slot, rows] = value
            else:
                w[slot, rows] = value
            return carry

        lax.fori_loop(0, size // span, chunk, 0)

    def gather(slot, st):
        v, base = bases[slot]
        size = sizes[st]
        rows = pl.ds(pl.multiple_of(base[st] + v[st] * size, size), size)
        out = []
        for step in (1, 2, 3):
            i = sem_at(slot, 5 - st, step)
            out.append(
                send(
                    w2.at[slot, rows], w2.at[slot, rows], sel_s.at[i], sel_r.at[i],
                    along(ORDERS[slot][st], step),
                )
            )
        return out

    def finish(copies):
        for copy in copies:
            copy.wait()

    for copy in load_f[:2]:
        copy.wait()
    finish(fin_copies[:2])
    run = [None] * 3
    build(0, 0, 24)
    run[0] = scatter(0, 0)
    build(1, 0, 26)
    run[1] = scatter(1, 0)
    finish(fin_copies[2:])
    build(2, 1, 26)
    run[2] = scatter(2, 0)

    load_rhs.wait()
    load_d.wait()
    for t in range(3):

        def split(i, carry, t=t):
            rows = pl.ds(pl.multiple_of(i * 128, 128), 128)
            value = jnp.zeros((128, COLS), F32)
            for j in range(8):
                block = rhs[pl.ds(pl.multiple_of(j * NB + i * 128, 128), 128), :]
                value = jnp.where(flag(t * 8 + j) > 0.5, block, value)
            high = value.astype(BF16)
            thl[rows, pl.ds(0, COLS)] = high
            thl[rows, pl.ds(COLS, COLS)] = (value - high.astype(F32)).astype(BF16)
            return carry

        lax.fori_loop(0, 8, split, 0)

        def solve(i, carry, t=t):
            rows = pl.ds(pl.multiple_of(i * 256, 256), 256)
            both = dot(diag[t, rows], thl[...])
            value = both[:, :COLS] + both[:, COLS:]
            high = value.astype(BF16)
            if t == 0:
                a0[rows] = value
                stage[0, rows] = high
            else:
                stage[2 * t - 1, rows] = high
                stage[2 * t, rows] = (value - high.astype(F32)).astype(BF16)
            return carry

        lax.fori_loop(0, 4, solve, 0)

    a_copy = send(stage.at[:, theirs], a_in, a_s.at[0], a_r.at[0], partner)
    a_copy.wait()
    for t in range(5):
        a_half[t] = stage[t, mine] + a_in[t]
    z_rows = [pl.ds(pl.multiple_of(((z + step) % 4) * 128, 128), 128) for step in range(4)]
    z_copies = [
        send(a_half.at[:, z_rows[step]], a_z.at[step - 1], a_s.at[step], a_r.at[step], along(2, step))
        for step in (1, 2, 3)
    ]

    for slot in range(3):
        total(slot, 0, run[slot])
        run[slot] = scatter(slot, 1)

    finish(z_copies)
    for t in range(5):
        a_piece[t] = a_half[t, z_rows[0]] + a_z[0, t] + (a_z[1, t] + a_z[2, t])
    y_copy = send(a_piece, a_y, a_s.at[4], a_r.at[4], along(1, 2))

    for slot in range(3):
        total(slot, 1, run[slot])
        run[slot] = scatter(slot, 2)

    y_copy.wait()
    piece = pl.ds(pl.multiple_of(core * HALF + z * 128, 128), 128)
    for t in range(5):
        afull[t, piece] = a_piece[t] + a_y[t]
    z_copies = [
        send(afull.at[:, piece], afull.at[:, piece], a_s.at[4 + step], a_r.at[4 + step], along(2, step))
        for step in (1, 2, 3)
    ]

    for slot in range(3):
        total(slot, 2, run[slot])
        run[slot] = gather(slot, 2)

    finish(z_copies)
    a_copy = send(afull.at[:, mine], afull.at[:, mine], a_s.at[8], a_r.at[8], partner)

    def publish(t, src):
        return [
            send(src, yf.at[t, gc, mine], y_s.at[t * 7 + i], y_r.at[t * 7 + i], (gr, row_peer(i, 1)))
            for i in range(7)
        ]

    def forward(t, i, copy):
        copy.wait()
        block = yf.at[t, row_peer(i, -1), mine]
        j = t * 7 + i
        return send(block, block, fw_s.at[j], fw_r.at[j], partner)

    y_copies = publish(0, afull.at[0, mine])

    for slot in range(3):
        finish(run[slot])
        run[slot] = gather(slot, 1)
    a_copy.wait()
    yf[0, gc] = afull[0]
    for slot in range(3):
        finish(run[slot])
        run[slot] = gather(slot, 0)

    forwards = [forward(0, i, y_copies[i]) for i in range(7)]
    finish(forwards)

    def contribute(t, first):
        keep = jnp.concatenate([flag(28 + t)] * 2, axis=1) > 0.5

        def pair(i, carry):
            right = jnp.concatenate([yf[t, 2 * i], yf[t, 2 * i + 1]], axis=1)

            def tile(m, inner):
                rows = pl.ds(pl.multiple_of(m * 256, 256), 256)
                value = dot(panel[t, rows], right)
                value = jnp.where(keep, value, jnp.zeros_like(value))
                for e in range(2):
                    part = value[:, e * COLS:(e + 1) * COLS]
                    acc[2 * i + e, rows] = part if first else acc[2 * i + e, rows] + part
                return inner

            lax.fori_loop(0, 4, tile, 0)
            return carry

        lax.fori_loop(0, 4, pair, 0)

    contribute(0, True)

    def product(slot, t, i):
        rows = pl.ds(pl.multiple_of(i * 256, 256), 256)
        low = pl.ds(pl.multiple_of(HALF + i * 256, 256), 256)
        return dot(w2[slot, rows], yf[t, gc, pl.ds(0, HALF)]) + dot(
            w2[slot, low], yf[t, gc, pl.ds(HALF, HALF)]
        )

    def exchange(n, g_out, g_in):
        copy = send(g_out.at[mine], g_in.at[mine], g_s.at[n], g_r.at[n], partner)
        copy.wait()

    def next_y(t, g_in):
        def tile(i, carry):
            rows = pl.ds(pl.multiple_of(i * 256, 256), 256)
            value = afull[2 * t - 1, rows].astype(F32) + afull[2 * t, rows].astype(F32)
            change = dot(diag[t, rows], g_in[...])
            for e in range(t):
                value = value - change[:, e * COLS:(e + 1) * COLS]
            ysol[t - 1, rows] = value
            yf[t, gc, rows] = value.astype(BF16)
            return carry

        lax.fori_loop(0, 4, tile, 0)

    def store_g(g_out, g_in, i, e, value):
        rows = pl.ds(pl.multiple_of(core * HALF + i * 256, 256), 256)
        short = value.astype(BF16)
        g_out[rows, pl.ds(e * COLS, COLS)] = short
        g_in[rows, pl.ds(e * COLS, COLS)] = short

    finish(run[0])
    for i in range(2):
        store_g(g0_out, g0_in, i, 0, product(0, 0, i))
    exchange(0, g0_out, g0_in)
    next_y(1, g0_in)
    y_copies = publish(1, yf.at[1, gc, mine])
    finish(run[1])
    finish(run[2])
    for i in range(2):
        store_g(g1_out, g1_in, i, 0, product(1, 0, i))
        store_g(g1_out, g1_in, i, 1, product(2, 1, i))
    exchange(1, g1_out, g1_in)
    next_y(2, g1_in)
    y2_copies = publish(2, yf.at[2, gc, mine])

    forwards = [forward(1, i, y_copies[i]) for i in range(7)]
    finish(forwards)
    contribute(1, False)

    load_f[2].wait()
    keep2 = flag(30) > 0.5

    def last(col, put):
        def tile(m, inner):
            rows = pl.ds(pl.multiple_of(m * 256, 256), 256)
            value = dot(panel[2, rows], yf[2, col])
            put(rows, (acc[col, rows] + jnp.where(keep2, value, jnp.zeros_like(value))).astype(BF16))
            return inner

        lax.fori_loop(0, 4, tile, 0)

    def put_own(rows, value):
        c_in[gc, rows] = value

    last(gc, put_own)
    c_copies = [None] * 7
    ahead = forward(2, 0, y2_copies[0])
    for i in range(7):
        arrived = ahead
        if i < 6:
            ahead = forward(2, i + 1, y2_copies[i + 1])
        arrived.wait()
        to = INVERSE[i]
        col = row_peer(i, -1)

        def put(rows, value, to=to):
            c_out[to, rows] = value

        last(col, put)
        c_copies[to] = send(c_out.at[to], c_in.at[gc], c_s.at[to], c_r.at[to], (gr, col))

    def settle(j):
        def tile(m, inner):
            rows = pl.ds(pl.multiple_of(j * NB + m * 256, 256), 256)
            part = pl.ds(pl.multiple_of(m * 256, 256), 256)
            value = rhs[rows, :] - c_in[j, part].astype(F32)
            for t, solved in enumerate((a0[part], ysol[0, part], ysol[1, part])):
                value = jnp.where(flags[pl.ds(t * 8 + j, 1), :] > 0.5, solved, value)
            rhs[rows, :] = value
            return inner

        lax.fori_loop(0, 4, tile, 0)
        rows = pl.ds(pl.multiple_of(j * NB, NB), NB)
        return rows

    stores = []
    rows = settle(gc)
    stores.append(local(rhs.at[rows], out_ref.at[rows], out_sem.at[7]))
    for i in range(7):
        c_copies[i].wait()
        rows = settle(row_peer(i, -1))
        stores.append(local(rhs.at[rows], out_ref.at[rows], out_sem.at[i]))
    finish(stores)


def shards(right_sides, factor_panel, diag_inverse, block_ids, step_blocks):
    gr, gc = lax.axis_index("gr"), lax.axis_index("gc")
    numbering = jnp.arange(128, dtype=jnp.int32)
    hit = block_ids[None, :] == step_blocks[:, None]
    place = jnp.sum(jnp.where(hit, numbering[None, :], 0), axis=1)
    own = place // 8 == gr
    inside = place % 8
    block = gr * 8 + gc
    beside = (gr + 1 - 2 * (gr % 2)) * 8 + gc
    my_id = jnp.sum(jnp.where(numbering == block, block_ids, 0))
    later = my_id > step_blocks
    chosen = own[:, None] & (inside[:, None] == numbering[None, :8])
    scalars = jnp.concatenate(
        [
            chosen.reshape(24),
            jnp.stack([place[1] == block, place[1] == beside, place[2] == block, place[2] == beside]),
            later,
            jnp.zeros((1,), bool),
        ]
    )
    flags = jnp.broadcast_to(scalars.astype(F32)[:, None], (32, COLS))
    dma = pltpu.SemaphoreType.DMA
    vm = pltpu.VMEM
    return pl.pallas_call(
        kernel,
        out_shape=jax.ShapeDtypeStruct((8 * NB, COLS), F32),
        in_specs=[pl.BlockSpec(memory_space=pltpu.VMEM)] + [pl.BlockSpec(memory_space=pl.ANY)] * 3,
        out_specs=pl.BlockSpec(memory_space=pl.ANY),
        scratch_shapes=[
            vm((8 * NB, COLS), F32),
            vm((3, NB, NB), BF16),
            vm((3, NB, NB), BF16),
            vm((2, NB, HALF), BF16),
            vm((3, NB, HALF), BF16),
            vm((3, NB, HALF), BF16),
            vm((3, 3, 256, HALF), BF16),
            vm((3, 3, 64, HALF), BF16),
            vm((3, 3, 16, HALF), BF16),
            vm((NB, 2 * COLS), BF16),
            vm((NB, COLS), F32),
            vm((5, NB, COLS), BF16),
            vm((5, HALF, COLS), BF16),
            vm((5, HALF, COLS), BF16),
            vm((3, 5, 128, COLS), BF16),
            vm((5, 128, COLS), BF16),
            vm((5, 128, COLS), BF16),
            vm((5, NB, COLS), BF16),
            vm((3, 8, NB, COLS), BF16),
            vm((2, NB, COLS), F32),
            vm((NB, COLS), BF16),
            vm((NB, COLS), BF16),
            vm((NB, 2 * COLS), BF16),
            vm((NB, 2 * COLS), BF16),
            vm((8, NB, COLS), F32),
            vm((7, NB, COLS), BF16),
            vm((8, NB, COLS), BF16),
            dma((5,)), dma((8,)),
            dma((4,)), dma((4,)),
            dma((54,)), dma((54,)),
            dma((9,)), dma((9,)),
            dma((21,)), dma((21,)),
            dma((21,)), dma((21,)),
            dma((2,)), dma((2,)),
            dma((7,)), dma((7,)),
        ],
        compiler_params=pltpu.CompilerParams(
            collective_id=0, has_side_effects=True, vmem_limit_bytes=60 << 20
        ),
        name="solve_steps",
    )(flags, right_sides, factor_panel, diag_inverse)


def solution(mesh):
    in_specs = (P("gr", "gc"), P(None, ("gr", "gc"), None), P(), P(), P())
    return jax.shard_map(shards, mesh=mesh, in_specs=in_specs, out_specs=P("gr", "gc"), check_vma=False)
```

time: 775 us -> 149 us (0.19)
  waiting for transfers between devices: 663 us -> 0 us
  Pallas kernels: 0 us -> 136 us
  matrix products: 31.6 us -> 0 us
  between operations: 21.3 us -> 2.6 us
  local copies, waits for them, and re-layouts: 23.4 us -> 5.96 us
  other arithmetic: 20.4 us -> 3.56 us
  starting transfers between devices: 13.2 us -> 0 us
    psum x3 -> x0, waiting for transfers between devices: 443 us -> none  [from_root(): return lax.psum(jnp.where(mine, shard, jnp.zeros_like(shard)), axis)]
    all_gather x3 -> x0, waiting for transfers between devices: 144 us -> none  [shards(): lax.all_gather(y_part.astype(jnp.bfloat16), 'gc', axis=1, tiled=True)]
    pallas_call x0 -> x1, Pallas kernels: none -> 136 us  [shards(): pl.pallas_call(kernel, out_shape=jax.ShapeDtypeStruct((8 * NB, COLS), F32...]
    all_to_all x3 -> x0, waiting for transfers between devices: 75.4 us -> none  [shards(): lax.all_to_all(contrib, 'gc', split_axis=1, concat_axis=0, tiled=True)]
    dot_general x6 -> x0, matrix products: 31.6 us -> none  [the longest x3 17.8 us: shards(): jnp.dot(panel_step, full_y.astype(jnp.bfloat16), preferred_element_type=j...]
    all_to_all x3 -> x0, starting transfers between devices: 12.8 us -> none  [shards(): lax.all_to_all(contrib, 'gc', split_axis=1, concat_axis=0, tiled=True)]
    unnamed x21 -> x1, local copies, waits for them, and re-layouts: 15.5 us -> 4.47 us
    select_n x6 -> x1, other arithmetic: 10.1 us -> 0.01 us  [shards(): inside = place % 8]
  transfers between devices with their start and end apart: 9 -> 0, of which waited for: 9 -> 0; matrix products, arithmetic and copies ran while one was open for 1% -> 0% of each run, Pallas kernels for 0% -> 0%
where the time goes in v1:
time: 149 us; the launch traced here: 148 us
  Pallas kernels  136 us (91%)
  local copies, waits for them, and re-layouts  5.96 us (4%)
  other arithmetic  3.56 us (2%)
  between operations  2.6 us (2%)
    pallas_call x1, Pallas kernels, shards(): pl.pallas_call(kernel, out_shape=jax.ShapeDtypeStruct((8 * NB, COLS), F32...  136 us
    unnamed x1, local copies, waits for them, and re-layouts  4.47 us

profile of v1, /device:TPU:0, one launch (start us, length us, event | category | flops | bytes accessed | tf_op | source)
XLA Modules:
  0.0 148.5 jit_solution(17492010236648338505)
XLA Ops:
  0.0 1.3 fusion
  1.3 1.3 broadcast_compare_fusion
  2.6 0.9 select_reduce_fusion
  3.5 0.1 compare_and_fusion
  3.6 0.1 and.50
  3.7 0.6 fusion.2
  6.8 0.1 concatenate.19
  7.0 0.7 broadcast_in_dim.31.flags
  7.6 136.4 %solve_steps.1 = f32[8192,128]{1,0:T(8,128)} custom-call(f32[32,128]{1,0:T(8,128)} %broadcast_in_dim.31.flags, f32[8192,128]{1,0:T(8,128)} %rhs_ref.1, bf16[3,1024,1024]{2,1,0:T(8,128)(2,1)} %panel_ref.1, bf16[3,1024,1024]{2,1,0:T(8,128)(2,1)} %diag_ref.1), custom_call_target="tpu_custom_call" | custom-call | tf_op jit(solution)/shard_map/solve_steps/pallas_call | solution.py:432
  144.0 4.5 %copy.7 = f32[8192,128]{1,0:T(8,128)} copy(f32[8192,128]{1,0:T(8,128)} %solve_steps.1) | data formatting | bytes 8388608
  (4 shorter events, 0.0 us)

commit v2 on v1

v2 whole, which is shorter than its diff:
```python
import jax
import jax.numpy as jnp
from jax import lax
from jax.experimental import pallas as pl
from jax.experimental.pallas import tpu as pltpu
from jax.sharding import PartitionSpec as P

MESH = pl.DeviceIdType.MESH
F32 = jnp.float32
BF16 = jnp.bfloat16
NB = 1024
HALF = 512
COLS = 128
ROW_PEERS = ((0, 1), (1, 0), (3, 0), (1, 1), (3, 1), (2, 0), (2, 1))
INVERSE = tuple(ROW_PEERS.index(((4 - dx) % 4, flip)) for dx, flip in ROW_PEERS)
ORDERS = ((0, 1, 2), (1, 2, 0), (2, 0, 1))


def dot(a, b):
    return jnp.dot(a, b, preferred_element_type=F32)


def kernel(
    steps_ref, ids_ref, rhs_ref, panel_ref, diag_ref, out_ref,
    flags, rhs, panel, diag, fin, w, fsl, r1, r2, r3,
    thl, a0, stage, a_in, a_half, a_z, a_piece, a_y, afull,
    yf, ysol, parts, g_full, acc, c_out, c_in,
    load_sem, out_sem, fin_s, fin_r, sel_s, sel_r, f_s, f_r, a_s, a_r,
    y_s, y_r, z_s, z_r, fw_s, fw_r, g_s, g_r, c_s, c_r,
):
    gr, gc = lax.axis_index("gr"), lax.axis_index("gc")
    z, y_hi, core = gr // 4, (gr // 2) % 2, gr % 2
    x, y_lo = gc // 2, gc % 2
    y = y_hi * 2 + y_lo
    other = 1 - core
    here = (x, y, z)

    def device(at, c):
        return (at[2] * 4 + (at[1] // 2) * 2 + c, at[0] * 2 + at[1] % 2)

    def along(axis, step):
        at = list(here)
        at[axis] = (at[axis] + step) % 4
        return device(at, core)

    def row_peer(i, sign):
        dx, flip = ROW_PEERS[i]
        return ((x + sign * dx + 4) % 4) * 2 + (y_lo + flip) % 2

    def send(src, dst, s, r, to):
        copy = pltpu.make_async_remote_copy(
            src_ref=src, dst_ref=dst, send_sem=s, recv_sem=r, device_id=to, device_id_type=MESH
        )
        copy.start()
        return copy

    def local(src, dst, sem):
        copy = pltpu.make_async_copy(src, dst, sem)
        copy.start()
        return copy

    partner = (gr + 1 - 2 * core, gc)
    mine = pl.ds(pl.multiple_of(core * HALF, HALF), HALF)
    theirs = pl.ds(pl.multiple_of(other * HALF, HALF), HALF)

    load_d = [local(diag_ref.at[0], diag.at[0], load_sem.at[0])]
    load_rhs = local(rhs_ref, rhs, load_sem.at[1])
    load_f = [local(panel_ref.at[t], panel.at[t], load_sem.at[2 + t]) for t in range(2)]
    load_d += [local(diag_ref.at[t], diag.at[t], load_sem.at[3 + t]) for t in (1, 2)]
    load_f.append(local(panel_ref.at[2], panel.at[2], load_sem.at[6]))

    group = [
        (((z + dz) % 4) * 4 + ((y_hi + dy) % 2) * 2 + (core + dk) % 2, gc)
        for dz in range(4) for dy in range(2) for dk in range(2)
    ][1:]
    peers = group + [(gr, row_peer(i, 1)) for i in range(7)]
    peers.append(device((x, (1 - y_hi) * 2 + 1 - y_lo, z), core))
    barrier = pltpu.get_barrier_semaphore()
    for peer in peers:
        pl.semaphore_signal(barrier, inc=1, device_id=peer, device_id_type=MESH)
    pl.semaphore_wait(barrier, len(peers))

    fin_copies = []
    for t in range(2):
        for h in range(2):
            i = t * 2 + h
            fin_copies.append(
                send(
                    panel_ref.at[t, theirs, pl.ds(h * HALF, HALF)],
                    fin.at[t, pl.ds(h * HALF, HALF)],
                    fin_s.at[i], fin_r.at[i], partner,
                )
            )

    lanes = lax.broadcasted_iota(jnp.int32, (1, 128), 1)
    ids = ids_ref[...]
    block = gr * 8 + gc
    beside = (gr + 1 - 2 * core) * 8 + gc
    my_id = jnp.sum(jnp.where(lanes == block, ids.astype(F32), 0.0), axis=1, keepdims=True)
    places = []
    for t in range(3):
        number = steps_ref[t]
        place = jnp.sum(jnp.where(ids == number, lanes.astype(F32), 0.0), axis=1, keepdims=True)
        places.append(jnp.broadcast_to(place, (1, 128)))
        pending = jnp.broadcast_to(my_id, (1, 128)).astype(jnp.int32) > number
        flags[28 + t:29 + t, :] = jnp.where(pending, 1.0, 0.0)
        for j in range(8):
            at = (gr * 8 + j).astype(F32)
            flags[t * 8 + j:t * 8 + j + 1, :] = jnp.where(places[t] == at, 1.0, 0.0)
    for row, t, at in ((24, 1, block), (25, 1, beside), (26, 2, block), (27, 2, beside)):
        flags[row:row + 1, :] = jnp.where(places[t] == at.astype(F32), 1.0, 0.0)

    def flag(row):
        return flags[row:row + 1, :]

    def build(slot, t, row):
        def mask(r):
            tile = jnp.broadcast_to(flag(r), (128, COLS)).astype(BF16)
            return jnp.concatenate([tile] * (HALF // COLS), axis=1)

        own, oth = mask(row), mask(row + 1)

        def chunk(i, carry):
            rows = pl.ds(pl.multiple_of(core * HALF + i * 128, 128), 128)
            for h in range(2):
                to = pl.ds(pl.multiple_of(h * HALF + i * 128, 128), 128)
                value = panel[t, rows, pl.ds(h * HALF, HALF)] * own + fin[t, to] * oth
                if slot == 0:
                    w[slot, to] = value
                else:
                    for m in range(8):
                        unit = pl.ds(pl.multiple_of(i * 256 + m * 32 + h * 16, 16), 16)
                        w[slot, unit] = value[m * 16:(m + 1) * 16]
            return carry

        lax.fori_loop(0, 4, chunk, 0)

    bases = []
    for slot in range(3):
        v = [here[a] for a in ORDERS[slot]]
        bases.append((v, (0, v[0] * 256, v[0] * 256 + v[1] * 64)))
    sizes = (256, 64, 16)

    def sem_at(slot, stage_no, step):
        return (slot * 3 + stage_no) * 3 + step - 1

    def scatter(slot, st):
        v, base = bases[slot]
        size = sizes[st]
        buf = (r1, r2, r3)[st]
        out = []
        for step in (1, 2, 3):
            rows = pl.ds(pl.multiple_of(base[st] + ((v[st] + step) % 4) * size, size), size)
            i = sem_at(slot, st, step)
            out.append(
                send(
                    w.at[slot, rows], buf.at[slot, step - 1], sel_s.at[i], sel_r.at[i],
                    along(ORDERS[slot][st], step),
                )
            )
        return out

    def total(slot, st, copies):
        v, base = bases[slot]
        size = sizes[st]
        buf = (r1, r2, r3)[st]
        for copy in copies:
            copy.wait()
        start = base[st] + v[st] * size
        span = min(size, 64)

        def chunk(i, carry):
            rows = pl.ds(pl.multiple_of(start + i * span, span), span)
            part = pl.ds(pl.multiple_of(i * span, span), span)
            value = w[slot, rows] + buf[slot, 0, part] + (buf[slot, 1, part] + buf[slot, 2, part])
            if st == 2:
                fsl[slot, gc] = value
            else:
                w[slot, rows] = value
            return carry

        lax.fori_loop(0, size // span, chunk, 0)

    def gather(slot):
        return [
            send(
                fsl.at[slot, gc], fsl.at[slot, gc], f_s.at[slot * 7 + i], f_r.at[slot * 7 + i],
                (gr, row_peer(i, 1)),
            )
            for i in range(7)
        ]

    def finish(copies):
        for copy in copies:
            copy.wait()

    def leading(t):
        def split(i, carry):
            rows = pl.ds(pl.multiple_of(i * 128, 128), 128)
            value = jnp.zeros((128, COLS), F32)
            for j in range(8):
                part = rhs[pl.ds(pl.multiple_of(j * NB + i * 128, 128), 128), :]
                value = jnp.where(flag(t * 8 + j) > 0.5, part, value)
            high = value.astype(BF16)
            thl[rows, pl.ds(0, COLS)] = high
            thl[rows, pl.ds(COLS, COLS)] = (value - high.astype(F32)).astype(BF16)
            return carry

        lax.fori_loop(0, 8, split, 0)

        def solve(i, carry):
            rows = pl.ds(pl.multiple_of(i * 256, 256), 256)
            both = dot(diag[t, rows], thl[...])
            value = both[:, :COLS] + both[:, COLS:]
            high = value.astype(BF16)
            if t == 0:
                a0[rows] = value
                stage[0, rows] = high
            else:
                stage[2 * t - 1, rows] = high
                stage[2 * t, rows] = (value - high.astype(F32)).astype(BF16)
            return carry

        lax.fori_loop(0, 4, solve, 0)

    spans = (pl.ds(0, 1), pl.ds(1, 4))
    members = (range(1), range(1, 5))
    z_rows = [pl.ds(pl.multiple_of(((z + step) % 4) * 128, 128), 128) for step in range(4)]
    piece = pl.ds(pl.multiple_of(core * HALF + z * 128, 128), 128)

    def a_sems(n, i):
        return a_s.at[n * 9 + i], a_r.at[n * 9 + i]

    def a_cores(n):
        return send(stage.at[spans[n], theirs], a_in.at[spans[n]], *a_sems(n, 0), partner)

    def a_join(n):
        for t in members[n]:
            a_half[t] = stage[t, mine] + a_in[t]

    def a_scatter(n):
        return [
            send(
                a_half.at[spans[n], z_rows[step]], a_z.at[step - 1, spans[n]],
                *a_sems(n, step), along(2, step),
            )
            for step in (1, 2, 3)
        ]

    def a_cross(n):
        for t in members[n]:
            a_piece[t] = a_half[t, z_rows[0]] + a_z[0, t] + (a_z[1, t] + a_z[2, t])
        return send(a_piece.at[spans[n]], a_y.at[spans[n]], *a_sems(n, 4), along(1, 2))

    def a_gather(n):
        for t in members[n]:
            afull[t, piece] = a_piece[t] + a_y[t]
        block_at = afull.at[spans[n], piece]
        return [
            send(block_at, block_at, *a_sems(n, 4 + step), along(2, step)) for step in (1, 2, 3)
        ]

    def a_share(n):
        block_at = afull.at[spans[n], mine]
        return send(block_at, block_at, *a_sems(n, 8), partner)

    def publish(t, rows):
        return [
            send(
                yf.at[t, gc, rows], yf.at[t, gc, rows], y_s.at[t * 7 + i], y_r.at[t * 7 + i],
                (gr, row_peer(i, 1)),
            )
            for i in range(7)
        ]

    def to_core(t, i):
        block_at = yf.at[t, row_peer(i, -1), mine]
        j = t * 7 + i
        return send(block_at, block_at, fw_s.at[j], fw_r.at[j], partner)

    run = [None] * 3
    load_d[0].wait()
    load_rhs.wait()
    leading(0)
    a_copy = a_cores(0)
    load_f[0].wait()
    finish(fin_copies[:2])
    build(0, 0, 24)
    run[0] = scatter(0, 0)
    build(1, 0, 26)
    run[1] = scatter(1, 0)
    a_copy.wait()
    a_join(0)
    z_copies = a_scatter(0)
    load_f[1].wait()
    finish(fin_copies[2:])
    build(2, 1, 26)
    run[2] = scatter(2, 0)
    for t in (1, 2):
        load_d[t].wait()
        leading(t)
    b_copy = a_cores(1)
    finish(z_copies)
    a_copy = a_cross(0)
    b_copy.wait()
    a_join(1)

    for slot in range(3):
        total(slot, 0, run[slot])
        run[slot] = scatter(slot, 1)
    a_copy.wait()
    z_copies = a_gather(0)
    b_copies = a_scatter(1)

    for slot in range(3):
        total(slot, 1, run[slot])
        run[slot] = scatter(slot, 2)
    finish(z_copies)
    a_copy = a_share(0)
    finish(b_copies)
    b_copy = a_cross(1)

    for slot in range(3):
        total(slot, 2, run[slot])
        run[slot] = gather(slot)
    a_copy.wait()
    yf[0, gc] = afull[0]
    y0_copies = publish(0, mine)
    b_copy.wait()
    b_copies = a_gather(1)

    def contribute(t):
        keep = jnp.concatenate([flag(28 + t)] * 2, axis=1) > 0.5

        def pair(i, carry):
            right = jnp.concatenate([yf[t, 2 * i], yf[t, 2 * i + 1]], axis=1)

            def tile(m, inner):
                rows = pl.ds(pl.multiple_of(m * 256, 256), 256)
                value = dot(panel[t, rows], right)
                value = jnp.where(keep, value, jnp.zeros_like(value))
                for e in range(2):
                    part = value[:, e * COLS:(e + 1) * COLS]
                    acc[2 * i + e, rows] = part
                return inner

            lax.fori_loop(0, 4, tile, 0)
            return carry

        lax.fori_loop(0, 4, pair, 0)

    lefts = ((0, 1, 2, 3), (0, 1, 4, 5), (0, 2, 4, 6))
    shift = (4, 2, 1)

    def product(n, t):
        low = jnp.concatenate([fsl[n, i] for i in lefts[n]], axis=0)
        high = jnp.concatenate([fsl[n, i + shift[n]] for i in lefts[n]], axis=0)
        value = dot(low, yf[t, gc, pl.ds(0, HALF)]) + dot(high, yf[t, gc, pl.ds(HALF, HALF)])
        parts[n, gr] = value.astype(BF16)
        return [
            send(parts.at[n, gr], parts.at[n, gr], g_s.at[n * 15 + i], g_r.at[n * 15 + i], group[i])
            for i in range(15)
        ]

    def unit_of(n, i, at_z, at_y):
        if n == 0:
            return (i >> 1) * 16 + at_y * 8 + (i & 1) * 4 + at_z
        if n == 1:
            return (at_y * 2 + (i & 1)) * 8 + at_z * 2 + (i >> 1)
        return at_z * 8 + i * 2 + at_y

    def assemble(n):
        for source in range(16):
            for i in range(4):
                unit = (source % 2) * 32 + unit_of(n, i, source // 4, (source // 2) % 2)
                g_full[pl.ds(unit * 16, 16), pl.ds((n // 2) * COLS, COLS)] = parts[
                    n, source, pl.ds(i * 16, 16)
                ]

    def next_y(t):
        def tile(i, carry):
            rows = pl.ds(pl.multiple_of(i * 256, 256), 256)
            value = afull[2 * t - 1, rows].astype(F32) + afull[2 * t, rows].astype(F32)
            change = dot(diag[t, rows], g_full[:, pl.ds(0, t * COLS)])
            for e in range(t):
                value = value - change[:, e * COLS:(e + 1) * COLS]
            ysol[t - 1, rows] = value
            yf[t, gc, rows] = value.astype(BF16)
            return carry

        lax.fori_loop(0, 4, tile, 0)

    finish(run[0])
    g_copies = [product(0, 0)]
    finish(run[1])
    g_copies.append(product(1, 0))
    finish(b_copies)
    b_copy = a_share(1)
    finish(g_copies[0])
    assemble(0)
    b_copy.wait()
    next_y(1)
    quarter = piece
    y1_copies = publish(1, quarter)
    finish(run[2])
    g_copies.append(product(2, 1))
    z_copies = []
    for i in range(7):
        y1_copies[i].wait()
        block_at = yf.at[1, row_peer(i, -1), quarter]
        z_copies.append(
            [
                send(block_at, block_at, z_s.at[i * 3 + step - 1], z_r.at[i * 3 + step - 1], along(2, step))
                for step in (1, 2, 3)
            ]
        )
    finish(g_copies[1])
    assemble(1)
    finish(g_copies[2])
    assemble(2)
    next_y(2)
    y2_copies = publish(2, mine)

    forwards = []
    for i in range(7):
        y0_copies[i].wait()
        forwards.append(to_core(0, i))
    finish(forwards)
    contribute(0)
    forwards1 = []
    for i in range(7):
        finish(z_copies[i])
        forwards1.append(to_core(1, i))

    load_f[2].wait()
    keep1, keep2 = flag(29) > 0.5, flag(30) > 0.5

    def last(col, put):
        def tile(m, inner):
            rows = pl.ds(pl.multiple_of(m * 256, 256), 256)
            value = acc[col, rows]
            for t, keep in ((1, keep1), (2, keep2)):
                change = dot(panel[t, rows], yf[t, col])
                value = value + jnp.where(keep, change, jnp.zeros_like(change))
            put(rows, value.astype(BF16))
            return inner

        lax.fori_loop(0, 4, tile, 0)

    def put_own(rows, value):
        c_in[gc, rows] = value

    last(gc, put_own)
    c_copies = [None] * 7
    y2_copies[0].wait()
    ahead = to_core(2, 0)
    for i in range(7):
        arrived = ahead
        if i < 6:
            y2_copies[i + 1].wait()
            ahead = to_core(2, i + 1)
        forwards1[i].wait()
        arrived.wait()
        to = INVERSE[i]
        col = row_peer(i, -1)

        def put(rows, value, to=to):
            c_out[to, rows] = value

        last(col, put)
        c_copies[to] = send(c_out.at[to], c_in.at[gc], c_s.at[to], c_r.at[to], (gr, col))

    def settle(j):
        def tile(m, inner):
            rows = pl.ds(pl.multiple_of(j * NB + m * 256, 256), 256)
            part = pl.ds(pl.multiple_of(m * 256, 256), 256)
            value = rhs[rows, :] - c_in[j, part].astype(F32)
            for t, solved in enumerate((a0[part], ysol[0, part], ysol[1, part])):
                value = jnp.where(flags[pl.ds(t * 8 + j, 1), :] > 0.5, solved, value)
            rhs[rows, :] = value
            return inner

        lax.fori_loop(0, 4, tile, 0)
        rows = pl.ds(pl.multiple_of(j * NB, NB), NB)
        return rows

    stores = []
    rows = settle(gc)
    stores.append(local(rhs.at[rows], out_ref.at[rows], out_sem.at[7]))
    for i in range(7):
        c_copies[i].wait()
        rows = settle(row_peer(i, -1))
        stores.append(local(rhs.at[rows], out_ref.at[rows], out_sem.at[i]))
    finish(stores)


def shards(right_sides, factor_panel, diag_inverse, block_ids, step_blocks):
    dma = pltpu.SemaphoreType.DMA
    vm = pltpu.VMEM
    return pl.pallas_call(
        kernel,
        out_shape=jax.ShapeDtypeStruct((8 * NB, COLS), F32),
        in_specs=[pl.BlockSpec(memory_space=pltpu.SMEM), pl.BlockSpec(memory_space=pltpu.VMEM)]
        + [pl.BlockSpec(memory_space=pl.ANY)] * 3,
        out_specs=pl.BlockSpec(memory_space=pl.ANY),
        scratch_shapes=[
            vm((32, COLS), F32),
            vm((8 * NB, COLS), F32),
            vm((3, NB, NB), BF16),
            vm((3, NB, NB), BF16),
            vm((2, NB, HALF), BF16),
            vm((3, NB, HALF), BF16),
            vm((3, 8, 16, HALF), BF16),
            vm((3, 3, 256, HALF), BF16),
            vm((3, 3, 64, HALF), BF16),
            vm((3, 3, 16, HALF), BF16),
            vm((NB, 2 * COLS), BF16),
            vm((NB, COLS), F32),
            vm((5, NB, COLS), BF16),
            vm((5, HALF, COLS), BF16),
            vm((5, HALF, COLS), BF16),
            vm((3, 5, 128, COLS), BF16),
            vm((5, 128, COLS), BF16),
            vm((5, 128, COLS), BF16),
            vm((5, NB, COLS), BF16),
            vm((3, 8, NB, COLS), BF16),
            vm((2, NB, COLS), F32),
            vm((3, 16, 64, COLS), BF16),
            vm((NB, 2 * COLS), BF16),
            vm((8, NB, COLS), F32),
            vm((7, NB, COLS), BF16),
            vm((8, NB, COLS), BF16),
            dma((7,)), dma((8,)),
            dma((4,)), dma((4,)),
            dma((27,)), dma((27,)),
            dma((21,)), dma((21,)),
            dma((18,)), dma((18,)),
            dma((21,)), dma((21,)),
            dma((21,)), dma((21,)),
            dma((21,)), dma((21,)),
            dma((45,)), dma((45,)),
            dma((7,)), dma((7,)),
        ],
        compiler_params=pltpu.CompilerParams(
            collective_id=0, has_side_effects=True, vmem_limit_bytes=60 << 20
        ),
        name="solve_steps",
    )(step_blocks, block_ids.reshape(1, 128), right_sides, factor_panel, diag_inverse)


def solution(mesh):
    in_specs = (P("gr", "gc"), P(None, ("gr", "gc"), None), P(), P(), P())
    return jax.shard_map(shards, mesh=mesh, in_specs=in_specs, out_specs=P("gr", "gc"), check_vma=False)
```

time: 149 us -> 129 us (0.87)
  Pallas kernels: 136 us -> 124 us
  other arithmetic: 3.56 us -> 0 us
  between operations: 2.6 us -> 0.01 us
  local copies, waits for them, and re-layouts: 5.96 us -> 4.47 us
    pallas_call x1, Pallas kernels: 136 us -> 124 us  [shards(): pl.pallas_call(kernel, out_shape=jax.ShapeDtypeStruct((8 * NB, COLS), F32...]
    reduce_sum x2 -> x0, other arithmetic: 2.14 us -> none  [the longest x1 1.29 us: shards(): my_id = jnp.sum(jnp.where(numbering == block, block_ids, 0))]
where the time goes in v2:
time: 129 us; the launch traced here: 128 us
  Pallas kernels  124 us (96%)
  local copies, waits for them, and re-layouts  4.47 us (3%)
    pallas_call x1, Pallas kernels, shards(): pl.pallas_call(kernel, out_shape=jax.ShapeDtypeStruct((8 * NB, COLS), F32...  124 us
    unnamed x1, local copies, waits for them, and re-layouts  4.47 us

profile of v2, /device:TPU:0, one launch (start us, length us, event | category | flops | bytes accessed | tf_op | source)
XLA Modules:
  0.0 128.3 jit_solution(16718309005597310419)
XLA Ops:
  0.0 123.8 %solve_steps.1 = f32[8192,128]{1,0:T(8,128)} custom-call(s32[3]{0:T(128)} %steps_ref.1, s32[1,128]{1,0:T(1,128)} %bitcast.1, f32[8192,128]{1,0:T(8,128)} %rhs_ref.1, bf16[3,1024,1024]{2,1,0:T(8,128)(2,1)} %panel_ref.1, bf16[3,1024,1024]{2,1,0:T(8,128)(2,1)} %diag_ref.1), custom_call_target="tpu_custom_call" | custom-call | tf_op jit(solution)/shard_map/solve_steps/pallas_call | solution.py:500
  123.8 4.5 %copy.7 = f32[8192,128]{1,0:T(8,128)} copy(f32[8192,128]{1,0:T(8,128)} %solve_steps.1) | data formatting | bytes 8388608

commit v3 on v2

v3 whole, which is shorter than its diff:
```python
import jax
import jax.numpy as jnp
from jax import lax
from jax.experimental import pallas as pl
from jax.experimental.pallas import tpu as pltpu
from jax.sharding import PartitionSpec as P

MESH = pl.DeviceIdType.MESH
F32 = jnp.float32
BF16 = jnp.bfloat16
NB = 1024
HALF = 512
COLS = 128
ROW_PEERS = ((2, 0), (1, 0), (3, 0), (0, 1), (2, 1), (1, 1), (3, 1))
ALONG_X = range(3)
DIRECT = range(4)
ACROSS = range(4, 7)
LAST = (3, 0, 4, 1, 5, 2, 6)
INVERSE = tuple(ROW_PEERS.index(((4 - dx) % 4, flip)) for dx, flip in ROW_PEERS)
ORDERS = ((0, 1, 2), (1, 2, 0), (2, 0, 1))


def dot(a, b):
    return jnp.dot(a, b, preferred_element_type=F32)


def kernel(
    steps_ref, ids_ref, rhs_ref, panel_ref, diag_ref, out_ref,
    flags, rhs, panel, diag, fin, w, fsl, r1, r2, r3,
    thl, a0, stage, a_in, a_half, a_z, a_piece, a_y, tst, t_in, t_half, t_z, t_piece, t_y,
    yf, ysol, g_full, c_out, c_in,
    load_sem, out_sem, fin_s, fin_r, sel_s, sel_r, f_s, f_r, a_s, a_r, t_s, t_r,
    y_s, y_r, z_s, z_r, fw_s, fw_r, g_s, g_r, h_s, h_r, c_s, c_r,
):
    gr, gc = lax.axis_index("gr"), lax.axis_index("gc")
    z, y_hi, core = gr // 4, (gr // 2) % 2, gr % 2
    x, y_lo = gc // 2, gc % 2
    y = y_hi * 2 + y_lo
    other = 1 - core
    here = (x, y, z)

    def device(at, c):
        return (at[2] * 4 + (at[1] // 2) * 2 + c, at[0] * 2 + at[1] % 2)

    def along(axis, step):
        at = list(here)
        at[axis] = (at[axis] + step) % 4
        return device(at, core)

    def row_peer(i, sign):
        dx, flip = ROW_PEERS[i]
        return ((x + sign * dx + 4) % 4) * 2 + (y_lo + flip) % 2

    def send(src, dst, s, r, to):
        copy = pltpu.make_async_remote_copy(
            src_ref=src, dst_ref=dst, send_sem=s, recv_sem=r, device_id=to, device_id_type=MESH
        )
        copy.start()
        return copy

    def local(src, dst, sem):
        copy = pltpu.make_async_copy(src, dst, sem)
        copy.start()
        return copy

    partner = (gr + 1 - 2 * core, gc)
    mine = pl.ds(pl.multiple_of(core * HALF, HALF), HALF)
    theirs = pl.ds(pl.multiple_of(other * HALF, HALF), HALF)

    load_d = [local(diag_ref.at[0], diag.at[0], load_sem.at[0])]
    load_rhs = local(rhs_ref, rhs, load_sem.at[1])
    load_f = [local(panel_ref.at[t], panel.at[t], load_sem.at[2 + t]) for t in range(2)]
    load_d += [local(diag_ref.at[t], diag.at[t], load_sem.at[3 + t]) for t in (1, 2)]
    load_f.append(local(panel_ref.at[2], panel.at[2], load_sem.at[6]))

    steps = [(dz, dy) for dz in range(4) for dy in range(2)][1:]
    group = [(((z + dz) % 4) * 4 + ((y_hi + dy) % 2) * 2 + core, gc) for dz, dy in steps]
    peers = group + [(gr, row_peer(i, 1)) for i in range(7)]
    peers += [device((x, (1 - y_hi) * 2 + 1 - y_lo, z), core), partner]
    barrier = pltpu.get_barrier_semaphore()
    for peer in peers:
        pl.semaphore_signal(barrier, inc=1, device_id=peer, device_id_type=MESH)
    pl.semaphore_wait(barrier, len(peers))

    fin_copies = []
    for t in range(2):
        for h in range(2):
            i = t * 2 + h
            fin_copies.append(
                send(
                    panel_ref.at[t, theirs, pl.ds(h * HALF, HALF)],
                    fin.at[t, pl.ds(h * HALF, HALF)],
                    fin_s.at[i], fin_r.at[i], partner,
                )
            )

    lanes = lax.broadcasted_iota(jnp.int32, (1, 128), 1)
    ids = ids_ref[...]
    block = gr * 8 + gc
    beside = (gr + 1 - 2 * core) * 8 + gc
    my_id = jnp.sum(jnp.where(lanes == block, ids.astype(F32), 0.0), axis=1, keepdims=True)
    places = []
    for t in range(3):
        number = steps_ref[t]
        place = jnp.sum(jnp.where(ids == number, lanes.astype(F32), 0.0), axis=1, keepdims=True)
        places.append(jnp.broadcast_to(place, (1, 128)))
        pending = jnp.broadcast_to(my_id, (1, 128)).astype(jnp.int32) > number
        flags[28 + t:29 + t, :] = jnp.where(pending, 1.0, 0.0)
        for j in range(8):
            at = (gr * 8 + j).astype(F32)
            flags[t * 8 + j:t * 8 + j + 1, :] = jnp.where(places[t] == at, 1.0, 0.0)
    for row, t, at in ((24, 1, block), (25, 1, beside), (26, 2, block), (27, 2, beside)):
        flags[row:row + 1, :] = jnp.where(places[t] == at.astype(F32), 1.0, 0.0)

    def flag(row):
        return flags[row:row + 1, :]

    def build(slot, t, row):
        def mask(r):
            tile = jnp.broadcast_to(flag(r), (128, COLS)).astype(BF16)
            return jnp.concatenate([tile] * (HALF // COLS), axis=1)

        own, oth = mask(row), mask(row + 1)

        def chunk(i, carry):
            rows = pl.ds(pl.multiple_of(core * HALF + i * 128, 128), 128)
            for h in range(2):
                to = pl.ds(pl.multiple_of(h * HALF + i * 128, 128), 128)
                value = panel[t, rows, pl.ds(h * HALF, HALF)] * own + fin[t, to] * oth
                for m in range(8):
                    at = (m % 2 * 2 + h, i, m // 2)
                    first, second, third = (at[a] for a in ORDERS[slot])
                    unit = pl.ds(pl.multiple_of((first * 16 + second * 4 + third) * 16, 16), 16)
                    w[slot, unit] = value[m * 16:(m + 1) * 16]
            return carry

        lax.fori_loop(0, 4, chunk, 0)

    bases = []
    for slot in range(3):
        v = [here[a] for a in ORDERS[slot]]
        bases.append((v, (0, v[0] * 256, v[0] * 256 + v[1] * 64)))
    sizes = (256, 64, 16)

    def sem_at(slot, stage_no, step):
        return (slot * 3 + stage_no) * 3 + step - 1

    def scatter(slot, st):
        v, base = bases[slot]
        size = sizes[st]
        buf = (r1, r2, r3)[st]
        out = []
        for step in (1, 2, 3):
            rows = pl.ds(pl.multiple_of(base[st] + ((v[st] + step) % 4) * size, size), size)
            i = sem_at(slot, st, step)
            out.append(
                send(
                    w.at[slot, rows], buf.at[slot, step - 1], sel_s.at[i], sel_r.at[i],
                    along(ORDERS[slot][st], step),
                )
            )
        return out

    def total(slot, st, copies):
        v, base = bases[slot]
        size = sizes[st]
        buf = (r1, r2, r3)[st]
        for copy in copies:
            copy.wait()
        start = base[st] + v[st] * size
        span = min(size, 64)

        def chunk(i, carry):
            rows = pl.ds(pl.multiple_of(start + i * span, span), span)
            part = pl.ds(pl.multiple_of(i * span, span), span)
            value = w[slot, rows] + buf[slot, 0, part] + (buf[slot, 1, part] + buf[slot, 2, part])
            if st == 2:
                fsl[slot, gc] = value
            else:
                w[slot, rows] = value
            return carry

        lax.fori_loop(0, size // span, chunk, 0)

    def gather(slot):
        return [
            send(
                fsl.at[slot, gc], fsl.at[slot, gc], f_s.at[slot * 7 + i], f_r.at[slot * 7 + i],
                (gr, row_peer(i, 1)),
            )
            for i in range(7)
        ]

    def finish(copies):
        for copy in copies:
            copy.wait()

    def target(t, i):
        value = jnp.zeros((128, COLS), F32)
        for j in range(8):
            part = rhs[pl.ds(pl.multiple_of(j * NB + i * 128, 128), 128), :]
            value = jnp.where(flag(t * 8 + j) > 0.5, part, value)
        high = value.astype(BF16)
        return high, (value - high.astype(F32)).astype(BF16)

    def leading():
        def split(i, carry):
            rows = pl.ds(pl.multiple_of(i * 128, 128), 128)
            thl[rows, pl.ds(0, COLS)], thl[rows, pl.ds(COLS, COLS)] = target(0, i)
            return carry

        lax.fori_loop(0, 8, split, 0)

        def solve(i, carry):
            rows = pl.ds(pl.multiple_of(i * 256, 256), 256)
            both = dot(diag[0, rows], thl[...])
            value = both[:, :COLS] + both[:, COLS:]
            a0[rows] = value
            stage[rows] = value.astype(BF16)
            return carry

        lax.fori_loop(0, 4, solve, 0)

    def later_targets():
        for t in (1, 2):
            def split(i, carry, t=t):
                for e, term in enumerate(target(t, i)):
                    for q in range(4):
                        tst[t * 2 - 2 + e, i, q] = term[q * 32:(q + 1) * 32]
                return carry

            lax.fori_loop(0, 8, split, 0)

    z_rows = [pl.ds(pl.multiple_of(((z + step) % 4) * 128, 128), 128) for step in range(4)]
    piece = pl.ds(pl.multiple_of(core * HALF + z * 128, 128), 128)

    def a_cores():
        return send(stage.at[theirs], a_in, a_s.at[0], a_r.at[0], partner)

    def a_scatter():
        a_half[...] = stage[mine] + a_in[...]
        return [
            send(a_half.at[z_rows[step]], a_z.at[step - 1], a_s.at[step], a_r.at[step], along(2, step))
            for step in (1, 2, 3)
        ]

    def a_cross():
        a_piece[...] = a_half[z_rows[0]] + a_z[0] + (a_z[1] + a_z[2])
        return send(a_piece, a_y, a_s.at[4], a_r.at[4], along(1, 2))

    def a_gather():
        yf[0, gc, piece] = a_piece[...] + a_y[...]
        block_at = yf.at[0, gc, piece]
        return [
            send(block_at, block_at, a_s.at[4 + step], a_r.at[4 + step], along(2, step))
            for step in (1, 2, 3)
        ]

    def a_share():
        block_at = yf.at[0, gc, mine]
        return send(block_at, block_at, a_s.at[8], a_r.at[8], partner)

    my_four = pl.ds(core * 4, 4)

    def t_cores():
        return send(tst.at[:, pl.ds(other * 4, 4)], t_in, t_s.at[0], t_r.at[0], partner)

    def t_scatter():
        for e in range(4):
            t_half[e] = tst[e, my_four] + t_in[e]
        return [
            send(
                t_half.at[:, :, (z + step) % 4], t_z.at[step - 1], t_s.at[step], t_r.at[step],
                along(2, step),
            )
            for step in (1, 2, 3)
        ]

    def t_cross():
        for e in range(4):
            t_piece[e] = t_half[e, :, z] + t_z[0, e] + (t_z[1, e] + t_z[2, e])
        return send(t_piece.at[:, pl.ds((1 - y_hi) * 2, 2)], t_y, t_s.at[4], t_r.at[4], along(1, 2))

    def t_own(t):
        value = jnp.zeros((2, 32, COLS), F32)
        for e in (2 * t - 2, 2 * t - 1):
            value = value + (t_piece[e, pl.ds(y_hi * 2, 2)] + t_y[e]).astype(F32)
        return value.reshape(64, COLS)

    def publish(t, which):
        copies = {}
        for i in which:
            rows = mine if i in DIRECT else piece
            block_at = yf.at[t, gc, rows]
            j = t * 7 + i
            copies[i] = send(block_at, block_at, y_s.at[j], y_r.at[j], (gr, row_peer(i, 1)))
        return copies

    def relay(t, copies):
        out = {}
        for i in ACROSS:
            copies[i].wait()
            block_at = yf.at[t, row_peer(i, -1), piece]
            j = (t * 3 + i - 4) * 3 - 1
            out[i] = [
                send(block_at, block_at, z_s.at[j + step], z_r.at[j + step], along(2, step))
                for step in (1, 2, 3)
            ]
        return out

    def arrive(copies, relays, i):
        if i in DIRECT:
            copies[i].wait()
        else:
            finish(relays[i])

    def to_core(t, i):
        block_at = yf.at[t, row_peer(i, -1), mine]
        j = t * 7 + i
        return send(block_at, block_at, fw_s.at[j], fw_r.at[j], partner)

    run = [None] * 3
    load_d[0].wait()
    load_rhs.wait()
    leading()
    a_copy = a_cores()
    load_f[0].wait()
    finish(fin_copies[:2])
    build(0, 0, 24)
    run[0] = scatter(0, 0)
    build(1, 0, 26)
    run[1] = scatter(1, 0)
    a_copy.wait()
    z_copies = a_scatter()
    load_f[1].wait()
    finish(fin_copies[2:])
    build(2, 1, 26)
    run[2] = scatter(2, 0)
    later_targets()
    t_copy = t_cores()
    finish(z_copies)
    a_copy = a_cross()

    for slot in range(3):
        total(slot, 0, run[slot])
        run[slot] = scatter(slot, 1)
    a_copy.wait()
    z_copies = a_gather()
    t_copy.wait()
    t_copies = t_scatter()

    for slot in range(3):
        total(slot, 1, run[slot])
        run[slot] = scatter(slot, 2)
    finish(z_copies)
    a_copy = a_share()
    finish(t_copies)
    t_copy = t_cross()

    for slot in range(3):
        total(slot, 2, run[slot])
        run[slot] = gather(slot)
    a_copy.wait()
    t_copy.wait()

    def product(slot, t):
        low = jnp.concatenate([fsl[slot, (i % 2) * 4 + i // 2] for i in range(4)], axis=0)
        high = jnp.concatenate([fsl[slot, (i % 2) * 4 + i // 2 + 2] for i in range(4)], axis=0)
        value = dot(low, yf[t, gc, pl.ds(0, HALF)]) + dot(high, yf[t, gc, pl.ds(HALF, HALF)])
        return value.astype(BF16).astype(F32)

    def spread(n, value):
        high = value.astype(BF16)
        both = jnp.concatenate([high, (value - high.astype(F32)).astype(BF16)], axis=1)
        for e in range(2):
            g_full[n, core, y_hi, e, z] = both[e * 32:(e + 1) * 32]
        block_at = g_full.at[n, core, y_hi, :, z]
        copies = [
            send(block_at, block_at, g_s.at[n * 7 + i], g_r.at[n * 7 + i], group[i]) for i in range(7)
        ]
        copies.append(send(block_at, block_at, h_s.at[n * 8 + 7], h_r.at[n * 8 + 7], partner))
        return copies

    def collect_spread(n, copies):
        shared = [copies[7]]
        for i, (dz, dy) in enumerate(steps):
            copies[i].wait()
            block_at = g_full.at[n, core, (y_hi + dy) % 2, :, (z + 4 - dz) % 4]
            shared.append(send(block_at, block_at, h_s.at[n * 8 + i], h_r.at[n * 8 + i], partner))
        finish(shared)

    def next_y(t):
        right = g_full[t - 1].reshape(NB, 2 * COLS)

        def tile(i, carry):
            rows = pl.ds(pl.multiple_of(i * 256, 256), 256)
            both = dot(diag[t, rows], right)
            value = both[:, :COLS] + both[:, COLS:]
            ysol[t - 1, rows] = value
            yf[t, gc, rows] = value.astype(BF16)
            return carry

        lax.fori_loop(0, 4, tile, 0)

    finish(run[0])
    s_copies = spread(0, t_own(1) - product(0, 0))
    y_copies = [publish(0, range(7)), None, None]
    relays = [None] * 3
    finish(run[1])
    second = t_own(2) - product(1, 0)
    load_d[1].wait()
    load_d[2].wait()
    collect_spread(0, s_copies)
    next_y(1)
    finish(run[2])
    s_copies = spread(1, second - product(2, 1))
    y_copies[1] = publish(1, range(7))
    relays[0] = relay(0, y_copies[0])
    collect_spread(1, s_copies)
    next_y(2)
    y_copies[2] = publish(2, (3, 4, 5, 6, 0, 1, 2))
    relays[1] = relay(1, y_copies[1])

    load_f[2].wait()
    keeps = [flag(28 + t) > 0.5 for t in range(3)]

    def last(col, put):
        def tile(m, inner):
            rows = pl.ds(pl.multiple_of(m * 256, 256), 256)
            value = jnp.zeros((256, COLS), F32)
            for t in range(3):
                change = dot(panel[t, rows], yf[t, col])
                value = value + jnp.where(keeps[t], change, jnp.zeros_like(change))
            put(rows, value.astype(BF16))
            return inner

        lax.fori_loop(0, 4, tile, 0)

    def put_own(rows, value):
        c_in[gc, rows] = value

    last(gc, put_own)
    c_copies = [None] * 7

    def collect(i):
        out = []
        for t in range(3):
            arrive(y_copies[t], relays[t], i)
            out.append(to_core(t, i))
        return out

    ahead = collect(LAST[0])
    relays[2] = relay(2, y_copies[2])
    for n, i in enumerate(LAST):
        arrived = ahead
        if n < 6:
            ahead = collect(LAST[n + 1])
        finish(arrived)
        to = INVERSE[i]
        col = row_peer(i, -1)

        def put(rows, value, to=to):
            c_out[to, rows] = value

        last(col, put)
        c_copies[to] = send(c_out.at[to], c_in.at[gc], c_s.at[to], c_r.at[to], (gr, col))

    def settle(j):
        def tile(m, inner):
            rows = pl.ds(pl.multiple_of(j * NB + m * 256, 256), 256)
            part = pl.ds(pl.multiple_of(m * 256, 256), 256)
            value = rhs[rows, :] - c_in[j, part].astype(F32)
            for t, solved in enumerate((a0[part], ysol[0, part], ysol[1, part])):
                value = jnp.where(flags[pl.ds(t * 8 + j, 1), :] > 0.5, solved, value)
            rhs[rows, :] = value
            return inner

        lax.fori_loop(0, 4, tile, 0)
        rows = pl.ds(pl.multiple_of(j * NB, NB), NB)
        return rows

    stores = []
    rows = settle(gc)
    stores.append(local(rhs.at[rows], out_ref.at[rows], out_sem.at[7]))
    for i in (INVERSE[n] for n in LAST):
        c_copies[i].wait()
        rows = settle(row_peer(i, -1))
        stores.append(local(rhs.at[rows], out_ref.at[rows], out_sem.at[i]))
    finish(stores)


def shards(right_sides, factor_panel, diag_inverse, block_ids, step_blocks):
    dma = pltpu.SemaphoreType.DMA
    vm = pltpu.VMEM
    return pl.pallas_call(
        kernel,
        out_shape=jax.ShapeDtypeStruct((8 * NB, COLS), F32),
        in_specs=[pl.BlockSpec(memory_space=pltpu.SMEM), pl.BlockSpec(memory_space=pltpu.VMEM)]
        + [pl.BlockSpec(memory_space=pl.ANY)] * 3,
        out_specs=pl.BlockSpec(memory_space=pl.ANY),
        scratch_shapes=[
            vm((32, COLS), F32),
            vm((8 * NB, COLS), F32),
            vm((3, NB, NB), BF16),
            vm((3, NB, NB), BF16),
            vm((2, NB, HALF), BF16),
            vm((3, NB, HALF), BF16),
            vm((3, 8, 16, HALF), BF16),
            vm((3, 3, 256, HALF), BF16),
            vm((3, 3, 64, HALF), BF16),
            vm((3, 3, 16, HALF), BF16),
            vm((NB, 2 * COLS), BF16),
            vm((NB, COLS), F32),
            vm((NB, COLS), BF16),
            vm((HALF, COLS), BF16),
            vm((HALF, COLS), BF16),
            vm((3, 128, COLS), BF16),
            vm((128, COLS), BF16),
            vm((128, COLS), BF16),
            vm((4, 8, 4, 32, COLS), BF16),
            vm((4, 4, 4, 32, COLS), BF16),
            vm((4, 4, 4, 32, COLS), BF16),
            vm((3, 4, 4, 32, COLS), BF16),
            vm((4, 4, 32, COLS), BF16),
            vm((4, 2, 32, COLS), BF16),
            vm((3, 8, NB, COLS), BF16),
            vm((2, NB, COLS), F32),
            vm((2, 2, 2, 2, 4, 32, 2 * COLS), BF16),
            vm((7, NB, COLS), BF16),
            vm((8, NB, COLS), BF16),
            dma((7,)), dma((8,)),
            dma((4,)), dma((4,)),
            dma((27,)), dma((27,)),
            dma((21,)), dma((21,)),
            dma((9,)), dma((9,)),
            dma((5,)), dma((5,)),
            dma((21,)), dma((21,)),
            dma((27,)), dma((27,)),
            dma((21,)), dma((21,)),
            dma((14,)), dma((14,)),
            dma((16,)), dma((16,)),
            dma((7,)), dma((7,)),
        ],
        compiler_params=pltpu.CompilerParams(
            collective_id=0, has_side_effects=True, vmem_limit_bytes=60 << 20
        ),
        name="solve_steps",
    )(step_blocks, block_ids.reshape(1, 128), right_sides, factor_panel, diag_inverse)


def solution(mesh):
    in_specs = (P("gr", "gc"), P(None, ("gr", "gc"), None), P(), P(), P())
    return jax.shard_map(shards, mesh=mesh, in_specs=in_specs, out_specs=P("gr", "gc"), check_vma=False)
```

time: 129 us -> 115 us (0.89)
  Pallas kernels: 124 us -> 110 us
    pallas_call x1, Pallas kernels: 124 us -> 110 us  [shards(): pl.pallas_call(kernel, out_shape=jax.ShapeDtypeStruct((8 * NB, COLS), F32...]
where the time goes in v3:
time: 115 us; the launch traced here: 114 us
  Pallas kernels  110 us (96%)
  local copies, waits for them, and re-layouts  4.47 us (4%)
    pallas_call x1, Pallas kernels, shards(): pl.pallas_call(kernel, out_shape=jax.ShapeDtypeStruct((8 * NB, COLS), F32...  110 us
    unnamed x1, local copies, waits for them, and re-layouts  4.47 us

profile of v3, /device:TPU:0, one launch (start us, length us, event | category | flops | bytes accessed | tf_op | source)
XLA Modules:
  0.0 114.1 jit_solution(11186177495073816145)
XLA Ops:
  0.0 109.6 %solve_steps.1 = f32[8192,128]{1,0:T(8,128)} custom-call(s32[3]{0:T(128)} %steps_ref.1, s32[1,128]{1,0:T(1,128)} %bitcast.1, f32[8192,128]{1,0:T(8,128)} %rhs_ref.1, bf16[3,1024,1024]{2,1,0:T(8,128)(2,1)} %panel_ref.1, bf16[3,1024,1024]{2,1,0:T(8,128)(2,1)} %diag_ref.1), custom_call_target="tpu_custom_call" | custom-call | tf_op jit(solution)/shard_map/solve_steps/pallas_call | solution.py:495
  109.6 4.5 %copy.7 = f32[8192,128]{1,0:T(8,128)} copy(f32[8192,128]{1,0:T(8,128)} %solve_steps.1) | data formatting | bytes 8388608

commit v4 on v3

--- a/solution.py
+++ b/solution.py
@@ -17,7 +17,10 @@
 ACROSS = range(4, 7)
 LAST = (3, 0, 4, 1, 5, 2, 6)
 INVERSE = tuple(ROW_PEERS.index(((4 - dx) % 4, flip)) for dx, flip in ROW_PEERS)
-ORDERS = ((0, 1, 2), (1, 2, 0), (2, 0, 1))
+ORDERS = ((0, 1, 2), (1, 2, 0), (2, 0, 1)) * 2
+BLOCK = (0, 0, 1, 1, 2, 2)
+FIRST, SECOND = range(3), range(3, 6)
+WIDE = 256
 
 
 def dot(a, b):
@@ -115,10 +118,12 @@
     def flag(row):
         return flags[row:row + 1, :]
 
-    def build(slot, t, row):
+    def build(part, t, row):
+        col = part % 2 * WIDE
+
         def mask(r):
             tile = jnp.broadcast_to(flag(r), (128, COLS)).astype(BF16)
-            return jnp.concatenate([tile] * (HALF // COLS), axis=1)
+            return jnp.concatenate([tile] * (WIDE // COLS), axis=1)
 
         own, oth = mask(row), mask(row + 1)
 
@@ -126,43 +131,46 @@
             rows = pl.ds(pl.multiple_of(core * HALF + i * 128, 128), 128)
             for h in range(2):
                 to = pl.ds(pl.multiple_of(h * HALF + i * 128, 128), 128)
-                value = panel[t, rows, pl.ds(h * HALF, HALF)] * own + fin[t, to] * oth
+                value = (
+                    panel[t, rows, pl.ds(h * HALF + col, WIDE)] * own
+                    + fin[t, to, pl.ds(col, WIDE)] * oth
+                )
                 for m in range(8):
                     at = (m % 2 * 2 + h, i, m // 2)
-                    first, second, third = (at[a] for a in ORDERS[slot])
+                    first, second, third = (at[a] for a in ORDERS[part])
                     unit = pl.ds(pl.multiple_of((first * 16 + second * 4 + third) * 16, 16), 16)
-                    w[slot, unit] = value[m * 16:(m + 1) * 16]
+                    w[part, unit] = value[m * 16:(m + 1) * 16]
             return carry
 
         lax.fori_loop(0, 4, chunk, 0)
 
     bases = []
-    for slot in range(3):
-        v = [here[a] for a in ORDERS[slot]]
+    for part in range(6):
+        v = [here[a] for a in ORDERS[part]]
         bases.append((v, (0, v[0] * 256, v[0] * 256 + v[1] * 64)))
     sizes = (256, 64, 16)
 
-    def sem_at(slot, stage_no, step):
-        return (slot * 3 + stage_no) * 3 + step - 1
-
-    def scatter(slot, st):
-        v, base = bases[slot]
+    def sem_at(part, stage_no, step):
+        return (part * 3 + stage_no) * 3 + step - 1
+
+    def scatter(part, st):
+        v, base = bases[part]
         size = sizes[st]
         buf = (r1, r2, r3)[st]
         out = []
         for step in (1, 2, 3):
             rows = pl.ds(pl.multiple_of(base[st] + ((v[st] + step) % 4) * size, size), size)
-            i = sem_at(slot, st, step)
+            i = sem_at(part, st, step)
             out.append(
                 send(
-                    w.at[slot, rows], buf.at[slot, step - 1], sel_s.at[i], sel_r.at[i],
-                    along(ORDERS[slot][st], step),
+                    w.at[part, rows], buf.at[part, step - 1], sel_s.at[i], sel_r.at[i],
+                    along(ORDERS[part][st], step),
                 )
             )
         return out
 
-    def total(slot, st, copies):
-        v, base = bases[slot]
+    def total(part, st, copies):
+        v, base = bases[part]
         size = sizes[st]
         buf = (r1, r2, r3)[st]
         for copy in copies:
@@ -172,12 +180,12 @@
 
         def chunk(i, carry):
             rows = pl.ds(pl.multiple_of(start + i * span, span), span)
-            part = pl.ds(pl.multiple_of(i * span, span), span)
-            value = w[slot, rows] + buf[slot, 0, part] + (buf[slot, 1, part] + buf[slot, 2, part])
+            some = pl.ds(pl.multiple_of(i * span, span), span)
+            value = w[part, rows] + buf[part, 0, some] + (buf[part, 1, some] + buf[part, 2, some])
             if st == 2:
-                fsl[slot, gc] = value
+                fsl[BLOCK[part], gc, :, pl.ds(part % 2 * WIDE, WIDE)] = value
             else:
-                w[slot, rows] = value
+                w[part, rows] = value
             return carry
 
         lax.fori_loop(0, size // span, chunk, 0)
@@ -221,15 +229,14 @@
 
         lax.fori_loop(0, 4, solve, 0)
 
-    def later_targets():
-        for t in (1, 2):
-            def split(i, carry, t=t):
-                for e, term in enumerate(target(t, i)):
-                    for q in range(4):
-                        tst[t * 2 - 2 + e, i, q] = term[q * 32:(q + 1) * 32]
-                return carry
-
-            lax.fori_loop(0, 8, split, 0)
+    def later_targets(t):
+        def split(i, carry):
+            for e, term in enumerate(target(t, i)):
+                for q in range(4):
+                    tst[t * 2 - 2 + e, i, q] = term[q * 32:(q + 1) * 32]
+            return carry
+
+        lax.fori_loop(0, 8, split, 0)
 
     z_rows = [pl.ds(pl.multiple_of(((z + step) % 4) * 128, 128), 128) for step in range(4)]
     piece = pl.ds(pl.multiple_of(core * HALF + z * 128, 128), 128)
@@ -262,24 +269,32 @@
 
     my_four = pl.ds(core * 4, 4)
 
-    def t_cores():
-        return send(tst.at[:, pl.ds(other * 4, 4)], t_in, t_s.at[0], t_r.at[0], partner)
-
-    def t_scatter():
-        for e in range(4):
+    def t_sems(t, i):
+        return t_s.at[t * 5 - 5 + i], t_r.at[t * 5 - 5 + i]
+
+    def terms(t):
+        return pl.ds(t * 2 - 2, 2)
+
+    def t_cores(t):
+        return send(tst.at[terms(t), pl.ds(other * 4, 4)], t_in.at[terms(t)], *t_sems(t, 0), partner)
+
+    def t_scatter(t):
+        for e in (2 * t - 2, 2 * t - 1):
             t_half[e] = tst[e, my_four] + t_in[e]
         return [
             send(
-                t_half.at[:, :, (z + step) % 4], t_z.at[step - 1], t_s.at[step], t_r.at[step],
+                t_half.at[terms(t), :, (z + step) % 4], t_z.at[step - 1, terms(t)], *t_sems(t, step),
                 along(2, step),
             )
             for step in (1, 2, 3)
         ]
 
-    def t_cross():
-        for e in range(4):
+    def t_cross(t):
+        for e in (2 * t - 2, 2 * t - 1):
             t_piece[e] = t_half[e, :, z] + t_z[0, e] + (t_z[1, e] + t_z[2, e])
-        return send(t_piece.at[:, pl.ds((1 - y_hi) * 2, 2)], t_y, t_s.at[4], t_r.at[4], along(1, 2))
+        return send(
+            t_piece.at[terms(t), pl.ds((1 - y_hi) * 2, 2)], t_y.at[terms(t)], *t_sems(t, 4), along(1, 2)
+        )
 
     def t_own(t):
         value = jnp.zeros((2, 32, COLS), F32)
@@ -319,49 +334,57 @@
         j = t * 7 + i
         return send(block_at, block_at, fw_s.at[j], fw_r.at[j], partner)
 
-    run = [None] * 3
+    run = [None] * 6
     load_d[0].wait()
     load_rhs.wait()
     leading()
     a_copy = a_cores()
     load_f[0].wait()
     finish(fin_copies[:2])
-    build(0, 0, 24)
-    run[0] = scatter(0, 0)
-    build(1, 0, 26)
-    run[1] = scatter(1, 0)
+    for part in FIRST:
+        build(part, 0, 24 if part < 2 else 26)
+        run[part] = scatter(part, 0)
     a_copy.wait()
     z_copies = a_scatter()
+    later_targets(1)
+    t_copy = t_cores(1)
+    build(3, 0, 26)
     load_f[1].wait()
     finish(fin_copies[2:])
-    build(2, 1, 26)
-    run[2] = scatter(2, 0)
-    later_targets()
-    t_copy = t_cores()
+    for part in (4, 5):
+        build(part, 1, 26)
     finish(z_copies)
     a_copy = a_cross()
 
-    for slot in range(3):
-        total(slot, 0, run[slot])
-        run[slot] = scatter(slot, 1)
+    for part in FIRST:
+        total(part, 0, run[part])
+        run[part] = scatter(part, 1)
+    for part in SECOND:
+        run[part] = scatter(part, 0)
+    t_copy.wait()
+    t_copies = t_scatter(1)
     a_copy.wait()
     z_copies = a_gather()
-    t_copy.wait()
-    t_copies = t_scatter()
-
-    for slot in range(3):
-        total(slot, 1, run[slot])
-        run[slot] = scatter(slot, 2)
+    later_targets(2)
+    t2_copy = t_cores(2)
+
+    for part in FIRST:
+        total(part, 1, run[part])
+        run[part] = scatter(part, 2)
     finish(z_copies)
     a_copy = a_share()
+    for part in (0, 1):
+        total(part, 2, run[part])
+    gathers = [gather(0), None, None]
+    total(2, 2, run[2])
     finish(t_copies)
-    t_copy = t_cross()
-
-    for slot in range(3):
-        total(slot, 2, run[slot])
-        run[slot] = gather(slot)
-    a_copy.wait()
-    t_copy.wait()
+    t_copy = t_cross(1)
+
+    for part in SECOND:
+        total(part, 0, run[part])
+        run[part] = scatter(part, 1)
+    t2_copy.wait()
+    t_copies = t_scatter(2)
 
     def product(slot, t):
         low = jnp.concatenate([fsl[slot, (i % 2) * 4 + i // 2] for i in range(4)], axis=0)
@@ -381,13 +404,13 @@
         copies.append(send(block_at, block_at, h_s.at[n * 8 + 7], h_r.at[n * 8 + 7], partner))
         return copies
 
-    def collect_spread(n, copies):
+    def share_spread(n, copies):
         shared = [copies[7]]
         for i, (dz, dy) in enumerate(steps):
             copies[i].wait()
             block_at = g_full.at[n, core, (y_hi + dy) % 2, :, (z + 4 - dz) % 4]
             shared.append(send(block_at, block_at, h_s.at[n * 8 + i], h_r.at[n * 8 + i], partner))
-        finish(shared)
+        return shared
 
     def next_y(t):
         right = g_full[t - 1].reshape(NB, 2 * COLS)
@@ -402,21 +425,33 @@
 
         lax.fori_loop(0, 4, tile, 0)
 
-    finish(run[0])
+    for part in SECOND:
+        total(part, 1, run[part])
+        run[part] = scatter(part, 2)
+    a_copy.wait()
+    t_copy.wait()
+    finish(gathers[0])
     s_copies = spread(0, t_own(1) - product(0, 0))
+    for part in SECOND:
+        total(part, 2, run[part])
+    gathers[1:] = [gather(1), gather(2)]
+    finish(t_copies)
+    t_copy = t_cross(2)
+    shared = share_spread(0, s_copies)
     y_copies = [publish(0, range(7)), None, None]
     relays = [None] * 3
-    finish(run[1])
-    second = t_own(2) - product(1, 0)
     load_d[1].wait()
     load_d[2].wait()
-    collect_spread(0, s_copies)
+    finish(shared)
     next_y(1)
-    finish(run[2])
+    t_copy.wait()
+    finish(gathers[1])
+    second = t_own(2) - product(1, 0)
+    finish(gathers[2])
     s_copies = spread(1, second - product(2, 1))
     y_copies[1] = publish(1, range(7))
     relays[0] = relay(0, y_copies[0])
-    collect_spread(1, s_copies)
+    finish(share_spread(1, s_copies))
     next_y(2)
     y_copies[2] = publish(2, (3, 4, 5, 6, 0, 1, 2))
     relays[1] = relay(1, y_copies[1])
@@ -439,7 +474,6 @@
     def put_own(rows, value):
         c_in[gc, rows] = value
 
-    last(gc, put_own)
     c_copies = [None] * 7
 
     def collect(i):
@@ -464,6 +498,8 @@
 
         last(col, put)
         c_copies[to] = send(c_out.at[to], c_in.at[gc], c_s.at[to], c_r.at[to], (gr, col))
+
+    last(gc, put_own)
 
     def settle(j):
         def tile(m, inner):
@@ -504,11 +540,11 @@
             vm((3, NB, NB), BF16),
             vm((3, NB, NB), BF16),
             vm((2, NB, HALF), BF16),
-            vm((3, NB, HALF), BF16),
+            vm((6, NB, WIDE), BF16),
             vm((3, 8, 16, HALF), BF16),
-            vm((3, 3, 256, HALF), BF16),
-            vm((3, 3, 64, HALF), BF16),
-            vm((3, 3, 16, HALF), BF16),
+            vm((6, 3, 256, WIDE), BF16),
+            vm((6, 3, 64, WIDE), BF16),
+            vm((6, 3, 16, WIDE), BF16),
             vm((NB, 2 * COLS), BF16),
             vm((NB, COLS), F32),
             vm((NB, COLS), BF16),
@@ -530,10 +566,10 @@
             vm((8, NB, COLS), BF16),
             dma((7,)), dma((8,)),
             dma((4,)), dma((4,)),
-            dma((27,)), dma((27,)),
+            dma((54,)), dma((54,)),
             dma((21,)), dma((21,)),
             dma((9,)), dma((9,)),
-            dma((5,)), dma((5,)),
+            dma((10,)), dma((10,)),
             dma((21,)), dma((21,)),
             dma((27,)), dma((27,)),
             dma((21,)), dma((21,)),

time: 115 us -> 113 us (0.983)
  Pallas kernels: 110 us -> 108 us
    pallas_call x1, Pallas kernels: 110 us -> 108 us  [shards(): pl.pallas_call(kernel, out_shape=jax.ShapeDtypeStruct((8 * NB, COLS), F32...]
where the time goes in v4:
time: 113 us
  Pallas kernels  108 us (96%)
  local copies, waits for them, and re-layouts  4.47 us (4%)
    pallas_call x1, Pallas kernels, shards(): pl.pallas_call(kernel, out_shape=jax.ShapeDtypeStruct((8 * NB, COLS), F32...  108 us
    unnamed x1, local copies, waits for them, and re-layouts  4.47 us

profile of v4, /device:TPU:0, one launch (start us, length us, event | category | flops | bytes accessed | tf_op | source)
XLA Modules:
  0.0 112.8 jit_solution(3412116291280132143)
XLA Ops:
  0.0 108.3 %solve_steps.1 = f32[8192,128]{1,0:T(8,128)} custom-call(s32[3]{0:T(128)} %steps_ref.1, s32[1,128]{1,0:T(1,128)} %bitcast.1, f32[8192,128]{1,0:T(8,128)} %rhs_ref.1, bf16[3,1024,1024]{2,1,0:T(8,128)(2,1)} %panel_ref.1, bf16[3,1024,1024]{2,1,0:T(8,128)(2,1)} %diag_ref.1), custom_call_target="tpu_custom_call" | custom-call | tf_op jit(solution)/shard_map/solve_steps/pallas_call | solution.py:531
  108.3 4.5 %copy.7 = f32[8192,128]{1,0:T(8,128)} copy(f32[8192,128]{1,0:T(8,128)} %solve_steps.1) | data formatting | bytes 8388608

commit v5 on v4

--- a/solution.py
+++ b/solution.py
@@ -12,10 +12,8 @@
 HALF = 512
 COLS = 128
 ROW_PEERS = ((2, 0), (1, 0), (3, 0), (0, 1), (2, 1), (1, 1), (3, 1))
-ALONG_X = range(3)
-DIRECT = range(4)
-ACROSS = range(4, 7)
-LAST = (3, 0, 4, 1, 5, 2, 6)
+DIRECT = ((0, 1, 2, 3), (0, 1, 2, 3), (0, 1, 2, 3))
+LAST = (3, 0, 5, 2, 4, 1, 6)
 INVERSE = tuple(ROW_PEERS.index(((4 - dx) % 4, flip)) for dx, flip in ROW_PEERS)
 ORDERS = ((0, 1, 2), (1, 2, 0), (2, 0, 1)) * 2
 BLOCK = (0, 0, 1, 1, 2, 2)
@@ -305,7 +303,7 @@
     def publish(t, which):
         copies = {}
         for i in which:
-            rows = mine if i in DIRECT else piece
+            rows = mine if i in DIRECT[t] else piece
             block_at = yf.at[t, gc, rows]
             j = t * 7 + i
             copies[i] = send(block_at, block_at, y_s.at[j], y_r.at[j], (gr, row_peer(i, 1)))
@@ -313,18 +311,20 @@
 
     def relay(t, copies):
         out = {}
-        for i in ACROSS:
+        for i in LAST:
+            if i in DIRECT[t]:
+                continue
             copies[i].wait()
             block_at = yf.at[t, row_peer(i, -1), piece]
-            j = (t * 3 + i - 4) * 3 - 1
+            j = (t * 7 + i) * 3 - 1
             out[i] = [
                 send(block_at, block_at, z_s.at[j + step], z_r.at[j + step], along(2, step))
                 for step in (1, 2, 3)
             ]
         return out
 
-    def arrive(copies, relays, i):
-        if i in DIRECT:
+    def arrive(t, copies, relays, i):
+        if i in DIRECT[t]:
             copies[i].wait()
         else:
             finish(relays[i])
@@ -453,7 +453,7 @@
     relays[0] = relay(0, y_copies[0])
     finish(share_spread(1, s_copies))
     next_y(2)
-    y_copies[2] = publish(2, (3, 4, 5, 6, 0, 1, 2))
+    y_copies[2] = publish(2, (3, 0, 4, 5, 6, 1, 2))
     relays[1] = relay(1, y_copies[1])
 
     load_f[2].wait()
@@ -479,12 +479,16 @@
     def collect(i):
         out = []
         for t in range(3):
-            arrive(y_copies[t], relays[t], i)
+            arrive(t, y_copies[t], relays[t], i)
             out.append(to_core(t, i))
         return out
 
-    ahead = collect(LAST[0])
-    relays[2] = relay(2, y_copies[2])
+    if LAST[0] in DIRECT[2]:
+        ahead = collect(LAST[0])
+        relays[2] = relay(2, y_copies[2])
+    else:
+        relays[2] = relay(2, y_copies[2])
+        ahead = collect(LAST[0])
     for n, i in enumerate(LAST):
         arrived = ahead
         if n < 6:
@@ -571,7 +575,7 @@
             dma((9,)), dma((9,)),
             dma((10,)), dma((10,)),
             dma((21,)), dma((21,)),
-            dma((27,)), dma((27,)),
+            dma((63,)), dma((63,)),
             dma((21,)), dma((21,)),
             dma((14,)), dma((14,)),
             dma((16,)), dma((16,)),

time: 113 us -> 110 us (0.973)
  Pallas kernels: 108 us -> 106 us
    pallas_call x1, Pallas kernels: 108 us -> 106 us  [shards(): pl.pallas_call(kernel, out_shape=jax.ShapeDtypeStruct((8 * NB, COLS), F32...]
where the time goes in v5:
time: 110 us
  Pallas kernels  106 us (96%)
  local copies, waits for them, and re-layouts  4.47 us (4%)
    pallas_call x1, Pallas kernels, shards(): pl.pallas_call(kernel, out_shape=jax.ShapeDtypeStruct((8 * NB, COLS), F32...  106 us
    unnamed x1, local copies, waits for them, and re-layouts  4.47 us

profile of v5, /device:TPU:0, one launch (start us, length us, event | category | flops | bytes accessed | tf_op | source)
XLA Modules:
  0.0 110.1 jit_solution(7877963672361316625)
XLA Ops:
  0.0 105.7 %solve_steps.1 = f32[8192,128]{1,0:T(8,128)} custom-call(s32[3]{0:T(128)} %steps_ref.1, s32[1,128]{1,0:T(1,128)} %bitcast.1, f32[8192,128]{1,0:T(8,128)} %rhs_ref.1, bf16[3,1024,1024]{2,1,0:T(8,128)(2,1)} %panel_ref.1, bf16[3,1024,1024]{2,1,0:T(8,128)(2,1)} %diag_ref.1), custom_call_target="tpu_custom_call" | custom-call | tf_op jit(solution)/shard_map/solve_steps/pallas_call | solution.py:535
  105.7 4.5 %copy.7 = f32[8192,128]{1,0:T(8,128)} copy(f32[8192,128]{1,0:T(8,128)} %solve_steps.1) | data formatting | bytes 8388608
